TPU v7x, 128 devices: a whole 4x4x4 slice. The times are simulated.
128 devices in a mesh: fsdp: 8 (over y, z_lo), tensor: 16 (over x, z_hi, core).
Axes of the slice: x: 4, y: 4, z: 4 (z_hi: 2, z_lo: 2; z = z_hi * 2 + z_lo), core: 2. Of those that a mesh axis runs over, the one named last changes fastest.
Arguments:
- inputs: bfloat16 [16384, 2048], P(('fsdp', 'tensor')), may hold values from -40 to 40
- gain: float32 [2048], replicated, may hold values from 0.1 to 1.9
- w_query: bfloat16 [2048, 4096], P('fsdp', 'tensor'), may hold values from -0.046875 to 0.046875
- w_key: bfloat16 [2048, 4096], P('fsdp', 'tensor'), may hold values from -0.046875 to 0.046875
- w_value: bfloat16 [2048, 4096], P('fsdp', 'tensor'), may hold values from -0.125 to 0.125
- w_out: bfloat16 [2048, 4096], P('fsdp', 'tensor'), may hold values from -0.125 to 0.125
- rel_bias: float32 [64, 32], P('tensor'), may hold values from -4 to 260
- d_output: bfloat16 [16384, 2048], P(('fsdp', 'tensor')), may hold values from -24 to 24
Outputs:
- d_inputs: bfloat16 [16384, 2048], P(('fsdp', 'tensor'))
- grad_query: float32 [2048, 4096], P('fsdp', 'tensor')
- grad_key: float32 [2048, 4096], P('fsdp', 'tensor')
- grad_value: float32 [2048, 4096], P('fsdp', 'tensor')
- grad_out: float32 [2048, 4096], P('fsdp', 'tensor')
All inputs are finite; a program needn't handle non-finite values.
Results may differ from a plain program's by a relative error of at most 0.017.
Values may be sent and summed in bfloat16 or wider, within the bound.
A program may use at most 128 MiB of HBM per device.

v0:
```python
import jax
import jax.numpy as jnp
import numpy as np
from jax import lax
from jax.sharding import PartitionSpec as P

BUCKETS = 32
MAX_DIST = 128
LEN = 256


epsilon = 1e-06


def bucket_grid(length, buckets, max_distance):
    positions = np.arange(length)
    relative = positions[None, :] - positions[:, None]
    half_count = buckets // 2
    exact_count = half_count // 2
    side_offset = np.where(relative > 0, half_count, 0)
    distance = np.abs(relative)
    log_ratio = np.log(np.maximum(distance, 1) / exact_count) / np.log(max_distance / exact_count)
    far_bucket = np.minimum(
        exact_count + np.floor(log_ratio * (half_count - exact_count)).astype(np.int64),
        half_count - 1,
    )
    return (side_offset + np.where(distance < exact_count, distance, far_bucket)).astype(np.int32)


def bias_grid(rel_bias, bucket_ids):
    expanded = jnp.zeros((rel_bias.shape[0],) + bucket_ids.shape, jnp.float32)
    for bucket in range(rel_bias.shape[1]):
        chosen = jnp.asarray(bucket_ids == bucket, jnp.float32)
        expanded = expanded + rel_bias[:, bucket][:, None, None] * chosen[None]
    return expanded


def per_device(inputs, gain, w_query, w_key, w_value, w_out, rel_bias, d_output):
    local_rows, width = inputs.shape
    total_rows = local_rows * lax.axis_size("tensor")
    length = LEN
    rows_pass = total_rows // length
    local_heads = rel_bias.shape[0]
    inner_local = w_query.shape[1]
    head_size = inner_local // local_heads
    flat_in = inputs.astype(jnp.float32)
    inv_rms = lax.rsqrt(jnp.mean(flat_in * flat_in, axis=-1, keepdims=True) + epsilon)
    unit_rows = flat_in * inv_rms
    normed = (unit_rows * gain).astype(jnp.bfloat16)
    w_query_all, w_key_all, w_value_all, w_out_all = (
        lax.all_gather(w_query, "fsdp", axis=0, tiled=True),
        lax.all_gather(w_key, "fsdp", axis=0, tiled=True),
        lax.all_gather(w_value, "fsdp", axis=0, tiled=True),
        lax.all_gather(w_out, "fsdp", axis=0, tiled=True),
    )
    normed_all = lax.all_gather(normed, "tensor", axis=0, tiled=True)

    def project(weight):
        return jnp.dot(normed_all, weight, preferred_element_type=jnp.float32).astype(jnp.bfloat16)

    def heads_view(array):
        return array.reshape(rows_pass, length, local_heads, head_size)

    query_rows = project(w_query_all)
    key_rows = project(w_key_all)
    value_rows = project(w_value_all)
    bias_full = bias_grid(rel_bias, bucket_grid(length, BUCKETS, MAX_DIST))
    scores = (
        jnp.einsum(
            "pihe,pjhe->phij",
            heads_view(query_rows),
            heads_view(key_rows),
            preferred_element_type=jnp.float32,
        )
        + bias_full[None]
    )
    row_max = jnp.max(scores, axis=-1, keepdims=True)
    exp_scores = jnp.exp(scores - row_max)
    attn_probs = exp_scores / jnp.sum(exp_scores, axis=-1, keepdims=True)
    probs_half = attn_probs.astype(jnp.bfloat16)
    context = (
        jnp.einsum(
            "phij,pjhe->pihe",
            probs_half,
            heads_view(value_rows),
            preferred_element_type=jnp.float32,
        )
        .astype(jnp.bfloat16)
        .reshape(total_rows, inner_local)
    )
    shard_rows = lax.all_gather(d_output, "tensor", axis=0, tiled=True)
    part_context = jnp.dot(shard_rows, w_out_all, preferred_element_type=jnp.float32).astype(
        jnp.bfloat16
    )
    term_sum = jnp.einsum("td,te->de", shard_rows, context, preferred_element_type=jnp.float32)
    d_heads = heads_view(part_context)
    d_prob = jnp.einsum(
        "pihe,pjhe->phij", d_heads, heads_view(value_rows), preferred_element_type=jnp.float32
    )
    d_value = (
        jnp.einsum("phij,pihe->pjhe", probs_half, d_heads, preferred_element_type=jnp.float32)
        .astype(jnp.bfloat16)
        .reshape(total_rows, inner_local)
    )
    row_dot = jnp.sum(attn_probs * d_prob, axis=-1, keepdims=True)
    d_score = (attn_probs * (d_prob - row_dot)).astype(jnp.bfloat16)
    d_query = (
        jnp.einsum(
            "phij,pjhe->pihe", d_score, heads_view(key_rows), preferred_element_type=jnp.float32
        )
        .astype(jnp.bfloat16)
        .reshape(total_rows, inner_local)
    )
    d_key = (
        jnp.einsum(
            "phij,pihe->pjhe", d_score, heads_view(query_rows), preferred_element_type=jnp.float32
        )
        .astype(jnp.bfloat16)
        .reshape(total_rows, inner_local)
    )
    grad_list = (d_query, d_key, d_value)
    running = jnp.zeros((local_rows * lax.axis_size("tensor"), width), jnp.float32)
    for gradient, weight in zip(grad_list, (w_query_all, w_key_all, w_value_all)):
        running = running + jnp.einsum(
            "te,de->td", gradient, weight, preferred_element_type=jnp.float32
        )
    d_normed = lax.psum_scatter(
        running.astype(jnp.bfloat16), "tensor", scatter_dimension=0, tiled=True
    ).astype(jnp.float32)
    stacked = lax.psum_scatter(
        jnp.concatenate(
            [
                jnp.einsum("td,te->de", normed_all, gradient, preferred_element_type=jnp.float32)
                for gradient in grad_list
            ]
            + [term_sum],
            axis=1,
        ).astype(jnp.bfloat16),
        "fsdp",
        scatter_dimension=0,
        tiled=True,
    ).astype(jnp.float32)
    grad_out = stacked[:, 3 * inner_local :]
    grad_query = stacked[:, :inner_local]
    grad_key = stacked[:, inner_local : 2 * inner_local]
    grad_value = stacked[:, 2 * inner_local : 3 * inner_local]
    d_unit = d_normed * gain
    branch = inv_rms * (d_unit - unit_rows * jnp.mean(d_unit * unit_rows, axis=-1, keepdims=True))
    d_inputs = (d_output.astype(jnp.float32) + branch).astype(jnp.bfloat16)
    return (d_inputs, grad_query, grad_key, grad_value, grad_out)


def solution(mesh):
    return jax.shard_map(
        per_device,
        mesh=mesh,
        in_specs=(
            P(("fsdp", "tensor"), None),
            P(),
            P("fsdp", "tensor"),
            P("fsdp", "tensor"),
            P("fsdp", "tensor"),
            P("fsdp", "tensor"),
            P("tensor", None),
            P(("fsdp", "tensor"), None),
        ),
        out_specs=(
            P(("fsdp", "tensor"), None),
            P("fsdp", "tensor"),
            P("fsdp", "tensor"),
            P("fsdp", "tensor"),
            P("fsdp", "tensor"),
        ),
        check_vma=False,
    )
```

profile of v0, /device:TPU:0, one launch (start us, length us, event | category | flops | bytes accessed | tf_op | source)
XLA Modules:
  0.0 589.0 jit_solution(18144623188056598948)
XLA Ops:
  7.9 1.2 fusion.33
  9.2 2.0 fusion.27
  13.8 1.6 slice_reduce_fusion.29
  15.3 1.9 slice_reduce_fusion.30
  17.2 7.1 %multiply_add_fusion = f32[4,256,256]{1,2,0:T(8,128)} fusion(f32[4]{0:T(128)S(1)} %get-tuple-element.29, f32[256,256]{0,1:T(8,128)} %constant.105.clone, f32[4]{0:T(128)S(1)} %get-tuple-element.45, f32[256,256]{0,1:T(8,128)} %constant.104.clone, f32[4]{0:T(128)S(1)} %get-tuple-element.46, f32[256,256]{0,1:T(8,128)} %constant.103.clone, ...), kind=kLoop, calls=%fused_computation.44 | loop fusion | flops 16252928 | bytes 9175552 | tf_op jit(solution)/shard_map/add | solution.py:34
  24.4 26.8 %all-gather.17.cloned.1.call-done = bf16[2048,256]{1,0:T(8,128)(2,1)} async-done(((bf16[256,256]{1,0:T(8,128)(2,1)}), bf16[2048,256]{1,0:T(8,128)(2,1)}) %all-gather.17.cloned.1.call-update) | async-done | bytes 1048592 | tf_op jit(solution)/shard_map/all_gather | solution.py:53
  51.2 75.6 %all-gather.7.cloned.1.call-done = bf16[2048,2048]{1,0:T(8,128)(2,1)} async-done(((bf16[128,2048]{1,0:T(8,128)(2,1)}), bf16[2048,2048]{1,0:T(8,128)(2,1)}) %all-gather.7.cloned.1.call-update) | async-done | bytes 8388624 | tf_op jit(solution)/shard_map/all_gather | solution.py:56
  126.8 6.0 %convolution_convert_fusion.4 = bf16[2048,256]{1,0:T(8,128)(2,1)S(1)} fusion(bf16[2048,2048]{1,0:T(8,128)(2,1)} %all-gather.7.cloned.1.call-done, bf16[2048,256]{1,0:T(8,128)(2,1)} %all-gather.17.cloned.1.call-done), kind=kOutput, calls=%fused_computation.14 | convolution fusion | flops 2148007936 | bytes 10485760 | tf_op jit(solution)/shard_map/dot_general | solution.py:59
  132.8 1.2 reshape.193
  134.0 2.2 copy.68
  136.2 29.0 %all-gather.11.cloned.1.call-done = bf16[2048,256]{1,0:T(8,128)(2,1)} async-done(((bf16[256,256]{1,0:T(8,128)(2,1)}), bf16[2048,256]{1,0:T(8,128)(2,1)}) %all-gather.11.cloned.1.call-update) | async-done | bytes 1048592 | tf_op jit(solution)/shard_map/all_gather | solution.py:51
  165.1 6.0 %convolution_convert_fusion.6 = bf16[2048,256]{1,0:T(8,128)(2,1)S(1)} fusion(bf16[2048,2048]{1,0:T(8,128)(2,1)} %all-gather.7.cloned.1.call-done, bf16[2048,256]{1,0:T(8,128)(2,1)} %all-gather.11.cloned.1.call-done), kind=kOutput, calls=%fused_computation.16 | convolution fusion | flops 2148007936 | bytes 10485760 | tf_op jit(solution)/shard_map/dot_general | solution.py:59
  171.1 0.9 reshape.191
  172.0 2.2 copy.63
  174.2 31.4 %all-gather.9.cloned.1.call-done = bf16[2048,256]{1,0:T(8,128)(2,1)} async-done(((bf16[256,256]{1,0:T(8,128)(2,1)}), bf16[2048,256]{1,0:T(8,128)(2,1)}) %all-gather.9.cloned.1.call-update) | async-done | bytes 1048592 | tf_op jit(solution)/shard_map/all_gather | solution.py:52
  205.6 6.0 %convolution_convert_fusion.7 = bf16[2048,256]{1,0:T(8,128)(2,1)S(1)} fusion(bf16[2048,2048]{1,0:T(8,128)(2,1)} %all-gather.7.cloned.1.call-done, bf16[2048,256]{1,0:T(8,128)(2,1)} %all-gather.9.cloned.1.call-done), kind=kOutput, calls=%fused_computation.17 | convolution fusion | flops 2148007936 | bytes 10485760 | tf_op jit(solution)/shard_map/dot_general | solution.py:59
  211.5 0.9 reshape.190
  212.4 1.0 copy.69
  213.4 32.6 %all-gather.15.cloned.1.call-done = bf16[2048,256]{1,0:T(8,128)(2,1)} async-done(((bf16[256,256]{1,0:T(8,128)(2,1)}), bf16[2048,256]{1,0:T(8,128)(2,1)}) %all-gather.15.cloned.1.call-update) | async-done | bytes 1048592 | tf_op jit(solution)/shard_map/all_gather | solution.py:54
  246.0 74.9 %all-gather.13.cloned.1.call-done = bf16[2048,2048]{1,0:T(8,128)(2,1)} async-done(((bf16[128,2048]{1,0:T(8,128)(2,1)}), bf16[2048,2048]{1,0:T(8,128)(2,1)}) %all-gather.13.cloned.1.call-update) | async-done | bytes 8388624 | tf_op jit(solution)/shard_map/all_gather | solution.py:91
  320.9 7.0 %convolution_convert_fusion.5 = bf16[2048,256]{1,0:T(8,128)(2,1)} fusion(bf16[2048,2048]{1,0:T(8,128)(2,1)} %all-gather.13.cloned.1.call-done, bf16[2048,256]{1,0:T(8,128)(2,1)} %all-gather.15.cloned.1.call-done), kind=kOutput, calls=%fused_computation.15 | convolution fusion | flops 2148007936 | bytes 10485760 | tf_op jit(solution)/shard_map/dot_general | solution.py:92
  327.9 3.3 reshape.192
  331.2 14.2 %copy.67 = bf16[8,256,4,64]{1,3,2,0:T(8,128)(2,1)} copy(bf16[8,256,4,64]{3,2,1,0:T(4,128)(2,1)S(1)} %reshape.192) | data formatting | bytes 2097152 | tf_op jit(solution)/shard_map/reshape | solution.py:62
  345.4 7.5 %fusion.37 = (f32[8,4,256]{2,1,0:T(4,128)S(1)}, f32[8,4,256,256]{2,3,1,0:T(8,128)}) fusion(f32[4,256,256]{1,2,0:T(8,128)} %multiply_add_fusion, bf16[8,256,4,64]{1,3,2,0:T(8,128)(2,1)} %copy.63, bf16[8,256,4,64]{1,3,2,0:T(8,128)(2,1)S(1)} %copy.69), kind=kOutput, calls=%fused_computation.81 | convolution fusion | flops 274727168 | bytes 11567104 | tf_op jit(solution)/shard_map/sub | solution.py:78
  352.9 4.9 fusion.21
  357.9 0.8 copy-done
  358.9 0.9 fusion.18
  359.9 1.8 multiply_reduce_fusion
  361.6 1.8 multiply_convert_fusion
  363.4 1.4 fusion.17
  364.8 0.9 fusion.16
  369.8 2.3 convolution_convert_fusion
  372.5 2.4 fusion.5
  374.9 2.3 convolution_convert_fusion.1
  377.2 2.5 convolution_convert_fusion.2
  379.8 2.4 pad_maximum_fusion
  382.2 9.7 %fusion.38 = f32[2048,2048]{1,0:T(8,128)} fusion(bf16[2048,256]{0,1:T(8,128)(2,1)S(1)} %bitcast.67, bf16[2048,256]{1,0:T(8,128)(2,1)} %all-gather.11.cloned.1.call-done), kind=kOutput, calls=%fused_computation.82 | convolution fusion | flops 2147483648 | bytes 18874368 | tf_op jit(solution)/shard_map/te,de->td/dot_general | solution.py:124
  391.9 8.1 %fusion.39 = f32[2048,2048]{1,0:T(8,128)} fusion(bf16[2048,256]{0,1:T(8,128)(2,1)S(1)} %bitcast.69, bf16[2048,256]{1,0:T(8,128)(2,1)S(1)} %copy-done.5), kind=kOutput, calls=%fused_computation.83 | convolution fusion | flops 2147483648 | bytes 18874368 | tf_op jit(solution)/shard_map/te,de->td/dot_general | solution.py:124
  400.0 15.7 %add_convert_fusion = bf16[2048,2048]{1,0:T(8,128)(2,1)} fusion(f32[2048,2048]{1,0:T(8,128)} %fusion.38, f32[2048,2048]{1,0:T(8,128)} %fusion.39, bf16[2048,256]{0,1:T(8,128)(2,1)S(1)} %bitcast.65, bf16[2048,256]{1,0:T(8,128)(2,1)S(1)} %copy-done.4), kind=kOutput, calls=%fused_computation.1 | convolution fusion | flops 2160066560 | bytes 44040192 | tf_op jit(solution)/shard_map/te,de->td/dot_general | solution.py:124
  415.7 54.5 %reduce-scatter.5.cloned.1.call-done = bf16[256,1024]{0,1:T(8,128)(2,1)} async-done(((bf16[2048,1024]{0,1:T(8,128)(2,1)}), bf16[256,1024]{0,1:T(8,128)(2,1)}) %reduce-scatter.5.cloned.1.call-update) | async-done | bytes 524304 | tf_op jit(solution)/shard_map/reduce_scatter | solution.py:130
  470.3 1.2 fusion.36
  471.4 0.8 copy.84
  472.3 0.8 copy.83
  473.1 0.8 copy.82
  474.0 0.8 copy.81
  474.8 103.5 %reduce-scatter.3.cloned.1.call-done = bf16[128,2048]{1,0:T(8,128)(2,1)} async-done(((bf16[2048,2048]{1,0:T(8,128)(2,1)}), bf16[128,2048]{1,0:T(8,128)(2,1)}) %reduce-scatter.3.cloned.1.call-update) | async-done | bytes 524304 | tf_op jit(solution)/shard_map/reduce_scatter | solution.py:127
  578.3 1.4 fusion.28
  579.7 2.2 fusion.32
  (53 shorter events, 8.0 us)
Async XLA Ops:
  7.2 44.0 %all-gather.17.cloned.1.call-start = ((), (), s32[]{:S(2)}) async-start(), calls=%async_computation.7 | async-start | bytes 1179648 | tf_op jit(solution)/shard_map/all_gather | solution.py:53
  7.9 118.9 %all-gather.7.cloned.1.call-start = ((), (), s32[]{:S(2)}) async-start(), calls=%async_computation.2 | async-start | bytes 8912896 | tf_op jit(solution)/shard_map/all_gather | solution.py:56
  11.2 153.9 %all-gather.11.cloned.1.call-start = ((), (), s32[]{:S(2)}) async-start(), calls=%async_computation.4 | async-start | bytes 1179648 | tf_op jit(solution)/shard_map/all_gather | solution.py:51
  12.0 193.6 %all-gather.9.cloned.1.call-start = ((), (), s32[]{:S(2)}) async-start(), calls=%async_computation.3 | async-start | bytes 1179648 | tf_op jit(solution)/shard_map/all_gather | solution.py:52
  12.6 233.4 %all-gather.15.cloned.1.call-start = ((), (), s32[]{:S(2)}) async-start(), calls=%async_computation.6 | async-start | bytes 1179648 | tf_op jit(solution)/shard_map/all_gather | solution.py:54
  13.1 307.8 %all-gather.13.cloned.1.call-start = ((), (), s32[]{:S(2)}) async-start(), calls=%async_computation.5 | async-start | bytes 8912896 | tf_op jit(solution)/shard_map/all_gather | solution.py:91
  13.7 456.5 %reduce-scatter.5.cloned.1.call-start = ((), (), s32[]{:S(2)}) async-start(), calls=%async_computation.9 | async-start | bytes 4718592 | tf_op jit(solution)/shard_map/reduce_scatter | solution.py:130
  345.4 7.5 %copy-start.7 = (bf16[8,256,4,64]{1,3,2,0:T(8,128)(2,1)S(1)}, bf16[8,256,4,64]{1,3,2,0:T(8,128)(2,1)}, u32[]{:S(2)}) copy-start(bf16[8,256,4,64]{1,3,2,0:T(8,128)(2,1)} %copy.67) | copy-start | bytes 3145732
  352.9 5.8 copy-start
  352.9 6.0 %copy-start.6 = (bf16[8,256,4,64]{1,3,2,0:T(8,128)(2,1)S(1)}, bf16[8,256,4,64]{1,3,2,0:T(8,128)(2,1)}, u32[]{:S(2)}) copy-start(bf16[8,256,4,64]{1,3,2,0:T(8,128)(2,1)} %copy.68) | copy-start | bytes 3145732
  361.6 1.8 copy-start.2
  365.7 3.7 slice-start
  367.5 2.3 slice-start.1
  369.0 3.1 slice-start.2
  369.8 2.8 slice-start.3
  382.1 196.1 %reduce-scatter.3.cloned.1.call-start = ((), (), s32[]{:S(2)}) async-start(), calls=%async_computation.8 | async-start | bytes 8912896 | tf_op jit(solution)/shard_map/reduce_scatter | solution.py:127
  382.2 9.7 %copy-start.5 = (bf16[2048,256]{1,0:T(8,128)(2,1)S(1)}, bf16[2048,256]{1,0:T(8,128)(2,1)}, u32[]{:S(2)}) copy-start(bf16[2048,256]{1,0:T(8,128)(2,1)} %all-gather.9.cloned.1.call-done) | copy-start | bytes 3145732
  391.9 8.1 %copy-start.4 = (bf16[2048,256]{1,0:T(8,128)(2,1)S(1)}, bf16[2048,256]{1,0:T(8,128)(2,1)}, u32[]{:S(2)}) copy-start(bf16[2048,256]{1,0:T(8,128)(2,1)} %all-gather.17.cloned.1.call-done) | copy-start | bytes 3145732
  415.7 162.6 %copy-start.1 = (bf16[128,2048]{1,0:T(8,128)(2,1)S(1)}, bf16[128,2048]{1,0:T(8,128)(2,1)}, u32[]{:S(2)}) copy-start(bf16[128,2048]{1,0:T(8,128)(2,1)} %param.40) | copy-start | bytes 1572868
  415.7 162.6 %copy-start.8 = (f32[2048]{0:T(1024)S(1)}, f32[2048]{0:T(1024)}, u32[]{:S(2)}) copy-start(f32[2048]{0:T(1024)} %param.41) | copy-start | bytes 24580
  415.7 164.0 %copy-start.3 = (bf16[128,2048]{1,0:T(8,128)(2,1)S(1)}, bf16[128,2048]{1,0:T(8,128)(2,1)}, u32[]{:S(2)}) copy-start(bf16[128,2048]{1,0:T(8,128)(2,1)} %param.47) | copy-start | bytes 1572868
Sparse Core Ops, SparseCore 0:
  9.6 41.4 all-gather.16
  54.1 72.6 all-gather.6
  128.4 36.6 all-gather.10
  166.6 38.8 all-gather.8
  207.1 38.8 all-gather.14
  248.2 72.6 all-gather.12
  382.3 87.9 reduce-scatter.4
  474.6 103.6 reduce-scatter.2
where the time goes:
time: 594 us; the launch traced here: 589 us
  waiting for transfers between devices  431 us (73%)
  matrix products  85.2 us (14%)
  local copies, waits for them, and re-layouts  37.5 us (6%)
  other arithmetic  20 us (3%)
  between operations  14.7 us (2%)
    reduce_scatter x1, waiting for transfers between devices, per_device(): lax.psum_scatter(running.astype(jnp.bfloat16), 'tensor', scatter_dimensio...  103 us
    all_gather x1, waiting for transfers between devices, per_device(): normed_all = lax.all_gather(normed, 'tensor', axis=0, tiled=True)  75.6 us
    all_gather x1, waiting for transfers between devices, per_device(): shard_rows = lax.all_gather(d_output, 'tensor', axis=0, tiled=True)  74.9 us
    reduce_scatter x1, waiting for transfers between devices, per_device(): lax.psum_scatter(jnp.concatenate([jnp.einsum('td,te->de', normed_all, gra...  54.5 us
    dot_general x3, matrix products, per_device(): jnp.einsum('te,de->td', gradient, weight, preferred_element_type=jnp.floa...  33.5 us
    all_gather x1, waiting for transfers between devices, per_device(): lax.all_gather(w_out, 'fsdp', axis=0, tiled=True)  32.6 us
    all_gather x1, waiting for transfers between devices, per_device(): lax.all_gather(w_key, 'fsdp', axis=0, tiled=True)  31.4 us
    all_gather x1, waiting for transfers between devices, per_device(): lax.all_gather(w_query, 'fsdp', axis=0, tiled=True)  29 us
  transfers between devices with their start and end apart: 8, of which 8 were waited for; matrix products, arithmetic and copies ran while one was open for 13% of the time, Pallas kernels for 0%

commit v1 on v0

v1 whole, which is shorter than its diff:
```python
import functools

import jax
import jax.numpy as jnp
import numpy as np
from jax import lax
from jax.experimental import pallas as pl
from jax.experimental.pallas import tpu as pltpu
from jax.sharding import PartitionSpec as P

BUCKETS = 32
MAX_DIST = 128
LEN = 256
EPSILON = 1e-06
MESH = pl.DeviceIdType.MESH
BF = jnp.bfloat16
F32 = jnp.float32
OUT, VAL, QRY, KEY = 0, 1, 2, 3


def bucket_steps():
    half_count = BUCKETS // 2
    exact_count = half_count // 2
    distance = np.arange(LEN)
    log_ratio = np.log(np.maximum(distance, 1) / exact_count) / np.log(MAX_DIST / exact_count)
    far = np.minimum(
        exact_count + np.floor(log_ratio * (half_count - exact_count)).astype(np.int64),
        half_count - 1,
    )
    bucket = np.where(distance < exact_count, distance, far)
    return [int(np.argmax(bucket >= k)) for k in range(half_count)]


def dot_nn(a, b):
    return lax.dot_general(a, b, (((1,), (0,)), ((), ())), preferred_element_type=F32)


def dot_nt(a, b):
    return lax.dot_general(a, b, (((1,), (1,)), ((), ())), preferred_element_type=F32)


class Links:
    def __init__(self, send_sem, recv_sem):
        self.send_sem, self.recv_sem = send_sem, recv_sem
        self.copies = {}

    def start(self, key, src, dst, peer):
        k = len(self.copies)
        copy = pltpu.make_async_remote_copy(
            src_ref=src,
            dst_ref=dst,
            send_sem=self.send_sem.at[k],
            recv_sem=self.recv_sem.at[k],
            device_id=peer,
            device_id_type=MESH,
        )
        copy.start()
        self.copies[key] = copy

    def arrived(self, *key):
        self.copies[key].wait_recv()

    def finish(self):
        for copy in self.copies.values():
            copy.wait_send()


N_COPIES = 136


def kernel(
    x_ref, gain_ref, wq_ref, wk_ref, wv_ref, wo_ref, rb_ref, do_ref,
    dx_ref, gq_ref, gk_ref, gv_ref, go_ref,
    tok, cot, wgt, rel, bias, heads, dheads, rows_t, part, sum1y, sum1z, sum2, dn, dn_sib, dn_x,
    splat, send_sem, recv_sem,
):
    f, t = lax.axis_index("fsdp"), lax.axis_index("tensor")
    x, zh, c = t // 4, (t // 2) % 2, t % 2
    y, zl = f // 2, f % 2
    z = zh * 2 + zl

    def dev(x, y, z, c):
        return (y * 2 + z % 2, (x * 2 + z // 2) * 2 + c)

    def xp(k):
        return (x + k) % 4

    def yp(k):
        return (y + k) % 4

    def zp(k):
        return (z + k) % 4

    sib = dev(x, y, z, 1 - c)
    to_x = {k: dev(xp(k), y, z, c) for k in (1, 2, 3)}
    to_y = {k: dev(x, yp(k), z, c) for k in (1, 2, 3)}
    to_z = {k: dev(x, y, zp(k), c) for k in (1, 2, 3)}
    peers = [sib] + list(to_x.values()) + list(to_y.values()) + list(to_z.values())
    barrier = pltpu.get_barrier_semaphore()
    for peer in peers:
        pl.semaphore_signal(barrier, inc=1, device_id=peer, device_id_type=MESH)
    pl.semaphore_wait(barrier, len(peers))

    net = Links(send_sem, recv_sem)

    def w_y(w, yy, zz, row, n):
        return wgt.at[w, zz // 2, yy, zz % 2, pl.ds(row, n)]

    def w_ycol(w, zz, row, n):
        return wgt.at[w, zz // 2, pl.ds(0, 4), zz % 2, pl.ds(row, n)]

    def w_zrow(w, yy, row, n):
        return wgt.at[w, pl.ds(0, 2), yy, pl.ds(0, 2), pl.ds(row, n)]

    for w, ref in ((OUT, wo_ref), (VAL, wv_ref), (QRY, wq_ref), (KEY, wk_ref)):
        wgt[w, zh, y, zl] = ref[...]
    rel[zh] = jnp.zeros((8, 128), F32)
    rel[zh, 0:4, 0:32] = rb_ref[...]
    cot[x, c] = do_ref[...]
    net.start(("rel",), rel.at[zh], rel.at[zh], to_z[2])

    def spread_own(name, buf):
        own = buf.at[x, c]
        net.start((name, 1), own, own, to_x[1])
        net.start((name, 3), own, own, to_x[3])
        net.start((name, "sib", 0), own, own, sib)

    spread_own("cot", cot)
    for w in range(4):
        a, b = w_y(w, y, z, 0, 128), w_y(w, y, z, 128, 128)
        net.start(("y", w, 1), a, a, to_y[1])
        net.start(("y", w, 3), a, a, to_y[3])
        net.start(("z", w, 1), b, b, to_z[1])
        net.start(("z", w, 3), b, b, to_z[3])

    def norm_rows(k):
        rows = x_ref[pl.ds(pl.multiple_of(k * 16, 16), 16), :].astype(F32)
        inv = lax.rsqrt(jnp.mean(rows * rows, axis=-1, keepdims=True) + EPSILON)
        return rows * inv, inv

    @pl.loop(0, 8)
    def _(k):
        unit, _ = norm_rows(k)
        tok[x, c, pl.ds(pl.multiple_of(k * 16, 16), 16), :] = (unit * gain_ref[...]).astype(BF)

    spread_own("tok", tok)

    for w in range(4):
        net.arrived("y", w, 1)
        s = w_y(w, yp(3), z, 0, 64)
        net.start(("yf", w, 1), s, s, to_y[1])
        net.arrived("z", w, 1)
        s = w_y(w, y, zp(3), 128, 64)
        net.start(("zf", w, 1), s, s, to_z[1])
        net.arrived("y", w, 3)
        s = w_y(w, yp(1), z, 64, 64)
        net.start(("yf", w, 3), s, s, to_y[3])
        net.arrived("z", w, 3)
        s = w_y(w, y, zp(1), 192, 64)
        net.start(("zf", w, 3), s, s, to_z[3])

    for w in range(4):
        net.arrived("yf", w, 1)
        net.arrived("yf", w, 3)
        s = w_ycol(w, z, 0, 128)
        net.start(("z2", w, 1), s, s, to_z[1])
        net.start(("z2", w, 3), s, s, to_z[3])
        net.arrived("zf", w, 1)
        net.arrived("zf", w, 3)
        s = w_zrow(w, y, 128, 128)
        net.start(("y2", w, 1), s, s, to_y[1])
        net.start(("y2", w, 3), s, s, to_y[3])

    net.arrived("rel")
    steps = bucket_steps()
    table = jnp.concatenate([rel[0, 0:4, :], rel[1, 0:4, :]], axis=0)
    for k in range(BUCKETS):
        splat[k] = jnp.broadcast_to(table[:, k : k + 1], (8, 128))

    @pl.loop(0, LEN // 8)
    def _(k):
        i = lax.broadcasted_iota(jnp.int32, (8, LEN), 0) + k * 8
        r = lax.broadcasted_iota(jnp.int32, (8, LEN), 1) - i
        values = [None] * 8

        def row(b, h):
            return jnp.broadcast_to(splat[b, h : h + 1, 0:1], (8, LEN))

        for h in range(8):
            values[h] = row(0, h)
        for b in range(1, BUCKETS // 2):
            chosen = r <= -steps[b]
            for h in range(8):
                values[h] = jnp.where(chosen, row(b, h), values[h])
        for b in range(1, BUCKETS // 2):
            chosen = r >= steps[b]
            for h in range(8):
                values[h] = jnp.where(chosen, row(BUCKETS // 2 + b, h), values[h])
        for h in range(8):
            bias[h, pl.ds(pl.multiple_of(k * 8, 8), 8), :] = values[h]

    def pass_tokens(name, buf):
        net.arrived(name, 1)
        s = buf.at[xp(3), c, pl.ds(0, 64)]
        net.start((name, "f", 1), s, s, to_x[1])
        s = buf.at[xp(3), c]
        net.start((name, "sib", 3), s, s, sib)
        net.arrived(name, 3)
        s = buf.at[xp(1), c, pl.ds(64, 64)]
        net.start((name, "f", 3), s, s, to_x[3])
        s = buf.at[xp(1), c]
        net.start((name, "sib", 1), s, s, sib)

    def pass_far(name, buf):
        net.arrived(name, "f", 1)
        net.arrived(name, "f", 3)
        s = buf.at[xp(2), c]
        net.start((name, "sib", 2), s, s, sib)

    def tokens_here(name):
        for k in range(4):
            net.arrived(name, "sib", k)

    def pass_weight(w):
        net.arrived("z2", w, 1)
        s = w_ycol(w, zp(3), 0, 64)
        net.start(("z2f", w, 1), s, s, to_z[1])
        net.arrived("y2", w, 1)
        s = w_zrow(w, yp(3), 128, 64)
        net.start(("y2f", w, 1), s, s, to_y[1])
        net.arrived("z2", w, 3)
        s = w_ycol(w, zp(1), 64, 64)
        net.start(("z2f", w, 3), s, s, to_z[3])
        net.arrived("y2", w, 3)
        s = w_zrow(w, yp(1), 192, 64)
        net.start(("y2f", w, 3), s, s, to_y[3])

    def weight_here(w):
        for name in ("z2f", "y2f"):
            net.arrived(name, w, 1)
            net.arrived(name, w, 3)

    def project(w, buf):
        @pl.loop(0, 4)
        def _(k):
            m, g = k // 2, k % 2
            left = buf[pl.ds(m * 2, 2)].reshape(512, 2048)
            right = wgt[w, g].reshape(2048, 256)
            heads[w, g, pl.ds(pl.multiple_of(m * 512, 512), 512), :] = dot_nn(left, right).astype(BF)

    pass_weight(OUT)
    pass_tokens("cot", cot)
    pass_weight(VAL)
    pass_tokens("tok", tok)
    pass_weight(QRY)
    pass_far("cot", cot)
    tokens_here("cot")
    weight_here(OUT)
    project(OUT, cot)
    pass_far("tok", tok)
    pass_weight(KEY)
    tokens_here("tok")
    weight_here(VAL)
    project(VAL, tok)
    weight_here(QRY)
    project(QRY, tok)
    weight_here(KEY)
    project(KEY, tok)

    lane = lax.broadcasted_iota(jnp.int32, (1, 128), 1)
    mask = [(lane < 64).astype(F32).astype(BF), (lane >= 64).astype(F32).astype(BF)]
    line = lax.broadcasted_iota(jnp.int32, (128, 1), 0)
    mask_t = [(line < 64).astype(F32).astype(BF), (line >= 64).astype(F32).astype(BF)]

    def attention(u):
        @pl.loop(0, 8)
        def _(k):
            p, g = k // 2, k % 2
            rows = pl.ds(pl.multiple_of(p * 256, 256), 256)
            lanes = pl.ds(u * 128, 128)
            dc2, v2, q2, k2 = (heads[w, g, rows, lanes] for w in range(4))
            probs_b, d_score = [], []
            for h in range(2):
                s = dot_nt(q2 * mask[h], k2) + bias[g * 4 + u * 2 + h]
                e = jnp.exp(s - jnp.max(s, axis=-1, keepdims=True))
                probs = e * (1.0 / jnp.sum(e, axis=-1, keepdims=True))
                d_prob = dot_nt(dc2 * mask[h], v2)
                row_dot = jnp.sum(probs * d_prob, axis=-1, keepdims=True)
                probs_b.append(probs.astype(BF))
                d_score.append((probs * (d_prob - row_dot)).astype(BF))
            ctx = dot_nn(
                jnp.concatenate(probs_b, axis=1),
                jnp.concatenate([v2 * mask[0], v2 * mask[1]], axis=0),
            ).astype(BF)
            dq = dot_nn(
                jnp.concatenate(d_score, axis=1),
                jnp.concatenate([k2 * mask[0], k2 * mask[1]], axis=0),
            ).astype(BF)
            dc_t, q_t = dc2.T, q2.T
            dv_t = dot_nn(
                jnp.concatenate([dc_t * mask_t[0], dc_t * mask_t[1]], axis=1),
                jnp.concatenate(probs_b, axis=0),
            ).astype(BF)
            dk_t = dot_nn(
                jnp.concatenate([q_t * mask_t[0], q_t * mask_t[1]], axis=1),
                jnp.concatenate(d_score, axis=0),
            ).astype(BF)
            cols = pl.ds(pl.multiple_of(p * 256, 256), 256)
            rows_t[u, OUT, g, :, cols] = ctx.T
            rows_t[u, VAL, g, :, cols] = dv_t
            rows_t[u, QRY, g, :, cols] = dq.T
            rows_t[u, KEY, g, :, cols] = dk_t
            dheads[VAL - 1, g, rows, lanes] = dv_t.T
            dheads[QRY - 1, g, rows, lanes] = dq
            dheads[KEY - 1, g, rows, lanes] = dk_t.T

    def weight_grads(u):
        @pl.loop(0, 8)
        def _(k):
            fy, fz = k // 2, k % 2
            cols = pl.ds(pl.multiple_of(k * 256, 256), 256)
            right = cot[:, :, :, cols].reshape(1024, 256)
            res = dot_nn(rows_t[u, OUT].reshape(256, 1024), right).astype(BF)
            part[u, OUT, :, fy, fz] = res.reshape(2, 128, 256)
            right = tok[:, :, :, cols].reshape(1024, 256)
            res = dot_nn(rows_t[u, 1:4].reshape(768, 1024), right).astype(BF)
            part[u, pl.ds(1, 3), :, fy, fz] = res.reshape(3, 2, 128, 256)

    def first_send(u, w):
        for j, k in enumerate((2, 1, 3)):
            if w in (OUT, VAL):
                src = part.at[u, w, pl.ds(0, 2), yp(k)]
                net.start(("s1", u, w, k), src, sum1y.at[u, w, j], to_y[k])
            else:
                src = part.at[u, w, zp(k) // 2, pl.ds(0, 4), zp(k) % 2]
                net.start(("s1", u, w, k), src, sum1z.at[u, w - 2, j], to_z[k])

    def first_sum(u, w):
        for k in (2, 1, 3):
            net.arrived("s1", u, w, k)
        for b in range(4):
            if w in (OUT, VAL):
                at = (u, w, b // 2, y, b % 2)
            else:
                at = (u, w, zh, b, zl)
            total = part[at].astype(F32)
            for j in range(3):
                other = sum1y[u, w, j, b // 2, b % 2] if w in (OUT, VAL) else sum1z[u, w - 2, j, b]
                total = total + other.astype(F32)
            part[at] = total.astype(BF)
        for j, k in enumerate((2, 1, 3)):
            if w in (OUT, VAL):
                src = part.at[u, w, zp(k) // 2, y, zp(k) % 2]
                net.start(("s2", u, w, k), src, sum2.at[u, w, j], to_z[k])
            else:
                src = part.at[u, w, zh, yp(k), zl]
                net.start(("s2", u, w, k), src, sum2.at[u, w, j], to_y[k])

    def second_sum(u, w, out):
        for k in (2, 1, 3):
            net.arrived("s2", u, w, k)
        total = part[u, w, zh, y, zl].astype(F32)
        for j in range(3):
            total = total + sum2[u, w, j].astype(F32)
        out[:, u * 128 : u * 128 + 128] = total.T

    attention(0)
    weight_grads(0)
    for w in range(4):
        first_send(0, w)
    attention(1)

    for k in (2, 1, 3, 0):
        p = xp(k)

        @pl.loop(0, 4)
        def _(n):
            left = [dheads[w, g, pl.ds(pl.multiple_of(p * 256, 256), 256), :] for w in range(3) for g in range(2)]
            right = [wgt[w + 1, g, n].reshape(512, 256) for w in range(3) for g in range(2)]
            total = dot_nt(left[0], right[0])
            for a, b in zip(left[1:], right[1:]):
                total = total + dot_nt(a, b)
            cols = pl.ds(pl.multiple_of(n * 512, 512), 512)
            dn[p, :, :, cols] = total.astype(BF).reshape(2, 128, 512)

        net.start(("dsib", k), dn.at[p, 1 - c], dn_sib.at[p], sib)

    weight_grads(1)
    for w in range(4):
        first_send(1, w)

    for k in (2, 1, 3, 0):
        p = xp(k)
        net.arrived("dsib", k)

        @pl.loop(0, 8)
        def _(m):
            rows = pl.ds(pl.multiple_of(m * 16, 16), 16)
            dn[p, c, rows, :] = (dn[p, c, rows, :].astype(F32) + dn_sib[p, rows, :].astype(F32)).astype(BF)

        if k:
            net.start(("dx", k), dn.at[p, c], dn_x.at[k - 1], to_x[k])

    outs = (go_ref, gv_ref, gq_ref, gk_ref)
    for u in range(2):
        for w in range(4):
            first_sum(u, w)
    for k in (2, 1, 3):
        net.arrived("dx", k)

    @pl.loop(0, 8)
    def _(m):
        rows = pl.ds(pl.multiple_of(m * 16, 16), 16)
        unit, inv = norm_rows(m)
        d_normed = dn[x, c, rows, :].astype(F32)
        for j in range(3):
            d_normed = d_normed + dn_x[j, rows, :].astype(F32)
        d_unit = d_normed * gain_ref[...]
        branch = inv * (d_unit - unit * jnp.mean(d_unit * unit, axis=-1, keepdims=True))
        dx_ref[rows, :] = (do_ref[rows, :].astype(F32) + branch).astype(BF)

    for u in range(2):
        for w in range(4):
            second_sum(u, w, outs[w])
    net.finish()


def per_device(inputs, gain, w_query, w_key, w_value, w_out, rel_bias, d_output):
    vmem = pl.BlockSpec(memory_space=pltpu.VMEM)
    grad = jax.ShapeDtypeStruct((256, 256), F32)
    return pl.pallas_call(
        kernel,
        out_shape=(jax.ShapeDtypeStruct((128, 2048), BF), grad, grad, grad, grad),
        in_specs=[vmem] * 8,
        out_specs=(vmem,) * 5,
        scratch_shapes=[
            pltpu.VMEM((4, 2, 128, 2048), BF),
            pltpu.VMEM((4, 2, 128, 2048), BF),
            pltpu.VMEM((4, 2, 4, 2, 256, 256), BF),
            pltpu.VMEM((2, 8, 128), F32),
            pltpu.VMEM((8, 256, 256), F32),
            pltpu.VMEM((4, 2, 1024, 256), BF),
            pltpu.VMEM((3, 2, 1024, 256), BF),
            pltpu.VMEM((2, 4, 2, 128, 1024), BF),
            pltpu.VMEM((2, 4, 2, 4, 2, 128, 256), BF),
            pltpu.VMEM((2, 2, 3, 2, 2, 128, 256), BF),
            pltpu.VMEM((2, 2, 3, 4, 128, 256), BF),
            pltpu.VMEM((2, 4, 3, 128, 256), BF),
            pltpu.VMEM((4, 2, 128, 2048), BF),
            pltpu.VMEM((4, 128, 2048), BF),
            pltpu.VMEM((3, 128, 2048), BF),
            pltpu.VMEM((32, 8, 128), F32),
            pltpu.SemaphoreType.DMA((N_COPIES,)),
            pltpu.SemaphoreType.DMA((N_COPIES,)),
        ],
        compiler_params=pltpu.CompilerParams(
            collective_id=0, has_side_effects=True, vmem_limit_bytes=62 * 1024 * 1024
        ),
        name="attention_backward",
    )(inputs, gain.reshape(1, -1), w_query, w_key, w_value, w_out, rel_bias, d_output)


def solution(mesh):
    return jax.shard_map(
        per_device,
        mesh=mesh,
        in_specs=(
            P(("fsdp", "tensor"), None),
            P(),
            P("fsdp", "tensor"),
            P("fsdp", "tensor"),
            P("fsdp", "tensor"),
            P("fsdp", "tensor"),
            P("tensor", None),
            P(("fsdp", "tensor"), None),
        ),
        out_specs=(
            P(("fsdp", "tensor"), None),
            P("fsdp", "tensor"),
            P("fsdp", "tensor"),
            P("fsdp", "tensor"),
            P("fsdp", "tensor"),
        ),
        check_vma=False,
    )
```

time: 594 us -> 142 us (0.24)
  waiting for transfers between devices: 431 us -> 0 us
  Pallas kernels: 0 us -> 133 us
  matrix products: 85.2 us -> 0 us
  local copies, waits for them, and re-layouts: 37.5 us -> 5.76 us
  other arithmetic: 20 us -> 0 us
  between operations: 14.7 us -> 0.66 us
    all_gather x6 -> x0, waiting for transfers between devices: 270 us -> none  [the longest x1 75.6 us: per_device(): normed_all = lax.all_gather(normed, 'tensor', axis=0, tiled=True)]
    reduce_scatter x2 -> x0, waiting for transfers between devices: 158 us -> none  [the longest x1 103 us: per_device(): lax.psum_scatter(running.astype(jnp.bfloat16), 'tensor', scatter_dimensio...]
    pallas_call x0 -> x1, Pallas kernels: none -> 133 us  [per_device(): pl.pallas_call(kernel, out_shape=(jax.ShapeDtypeStruct((128, 2048), BF),...]
    dot_general x16 -> x0, matrix products: 77.8 us -> none  [the longest x3 33.5 us: per_device(): jnp.einsum('te,de->td', gradient, weight, preferred_element_type=jnp.floa...]
    reshape x8 -> x0, local copies, waits for them, and re-layouts: 25.9 us -> none  [heads_view(): return array.reshape(rows_pass, length, local_heads, head_size)]
    sub x1 -> x0, matrix products: 7.48 us -> none  [per_device(): exp_scores = jnp.exp(scores - row_max)]
    add x1 -> x0, other arithmetic: 7.12 us -> none  [bias_grid(): expanded = expanded + rel_bias[:, bucket][:, None, None] * chosen[None]]
    convert_element_type x3 -> x0, other arithmetic: 6.03 us -> none  [the longest x1 2.25 us: per_device(): d_inputs = (d_output.astype(jnp.float32) + branch).astype(jnp.bfloat16)]
  transfers between devices with their start and end apart: 8 -> 0, of which waited for: 8 -> 0; matrix products, arithmetic and copies ran while one was open for 13% -> 0% of each run, Pallas kernels for 0% -> 0%
where the time goes in v1:
time: 142 us; the launch traced here: 140 us
  Pallas kernels  133 us (94%)
  local copies, waits for them, and re-layouts  5.76 us (4%)
    pallas_call x1, Pallas kernels, per_device(): pl.pallas_call(kernel, out_shape=(jax.ShapeDtypeStruct((128, 2048), BF),...  133 us
    unnamed x13, local copies, waits for them, and re-layouts  5.76 us

profile of v1, /device:TPU:0, one launch (start us, length us, event | category | flops | bytes accessed | tf_op | source)
XLA Modules:
  0.0 139.9 jit_solution(4101416604593205541)
XLA Ops:
  0.6 133.5 %attention_backward.1 = (bf16[128,2048]{1,0:T(8,128)(2,1)}, f32[256,256]{1,0:T(8,128)}, f32[256,256]{1,0:T(8,128)}, f32[256,256]{1,0:T(8,128)}, f32[256,256]{1,0:T(8,128)}) custom-call(bf16[128,2048]{1,0:T(8,128)(2,1)} %x_ref.1, f32[1,2048]{1,0:T(1,128)} %bitcast.1, bf16[256,256]{1,0:T(8,128)(2,1)} %wq_ref.1, bf16[256,256]{1,0:T(8,128)(2,1)} %wk_ref.1, ...), custom_call_target="tpu_custom_call" | custom-call | tf_op jit(solution)/shard_map/attention_backward/pallas_call | solution.py:431
  134.1 0.0 copy-start.3
  134.1 1.9 %copy.18 = bf16[128,2048]{1,0:T(8,128)(2,1)} copy(bf16[128,2048]{1,0:T(8,128)(2,1)} %get-tuple-element.10) | data formatting | bytes 1048576
  136.0 0.0 copy-done.3
  136.0 0.0 copy-start.2
  136.0 0.7 copy.19
  136.7 0.3 copy-done.2
  137.1 0.0 copy-start.1
  137.1 0.7 copy.20
  137.8 0.3 copy-done.1
  138.1 0.0 copy-start
  138.1 0.7 copy.21
  138.8 0.3 copy-done
  139.2 0.7 copy.22
Async XLA Ops:
  134.1 1.9 %copy-start.3 = (f32[256,256]{1,0:T(8,128)S(1)}, f32[256,256]{1,0:T(8,128)}, u32[]{:S(2)}) copy-start(f32[256,256]{1,0:T(8,128)} %get-tuple-element.11) | copy-start | bytes 786436
  136.0 1.0 copy-start.2
  137.1 1.0 copy-start.1
  138.1 1.0 copy-start

commit v2 on v0

v2 whole, which is shorter than its diff:
```python
import functools

import jax
import jax.numpy as jnp
import numpy as np
from jax import lax
from jax.experimental import pallas as pl
from jax.experimental.pallas import tpu as pltpu
from jax.sharding import PartitionSpec as P

BUCKETS = 32
MAX_DIST = 128
LEN = 256
EPSILON = 1e-06
MESH = pl.DeviceIdType.MESH
BF = jnp.bfloat16
F32 = jnp.float32
OUT, VAL, QRY, KEY = 0, 1, 2, 3


def bucket_steps():
    half_count = BUCKETS // 2
    exact_count = half_count // 2
    distance = np.arange(LEN)
    log_ratio = np.log(np.maximum(distance, 1) / exact_count) / np.log(MAX_DIST / exact_count)
    far = np.minimum(
        exact_count + np.floor(log_ratio * (half_count - exact_count)).astype(np.int64),
        half_count - 1,
    )
    bucket = np.where(distance < exact_count, distance, far)
    return [int(np.argmax(bucket >= k)) for k in range(half_count)]


def dot_nn(a, b):
    return lax.dot_general(a, b, (((1,), (0,)), ((), ())), preferred_element_type=F32)


def dot_nt(a, b):
    return lax.dot_general(a, b, (((1,), (1,)), ((), ())), preferred_element_type=F32)


class Links:
    def __init__(self, send_sem, recv_sem):
        self.send_sem, self.recv_sem = send_sem, recv_sem
        self.copies = {}

    def start(self, key, src, dst, peer):
        k = len(self.copies)
        copy = pltpu.make_async_remote_copy(
            src_ref=src,
            dst_ref=dst,
            send_sem=self.send_sem.at[k],
            recv_sem=self.recv_sem.at[k],
            device_id=peer,
            device_id_type=MESH,
        )
        copy.start()
        assert key not in self.copies
        self.copies[key] = copy

    def arrived(self, *key):
        self.copies[key].wait_recv()

    def finish(self):
        for copy in self.copies.values():
            copy.wait_send()


N_COPIES = 112


def kernel(
    x_ref, gain_ref, wq_ref, wk_ref, wv_ref, wo_ref, rb_ref, do_ref,
    dx_ref, gq_ref, gk_ref, gv_ref, go_ref,
    tok, cot, wgt, rel, bias, heads, dheads, rows_t,
    part_y, part_z, far_y, far_z, near_y, near_z, last,
    dn, dn_sib, far_x, near_x, splat, send_sem, recv_sem,
):
    f, t = lax.axis_index("fsdp"), lax.axis_index("tensor")
    x, zh, c = t // 4, (t // 2) % 2, t % 2
    y, zl = f // 2, f % 2
    z = zh * 2 + zl

    def dev(x, y, z, c):
        return (y * 2 + z % 2, (x * 2 + z // 2) * 2 + c)

    def xp(k):
        return (x + k) % 4

    def yp(k):
        return (y + k) % 4

    def zp(k):
        return (z + k) % 4

    sib = dev(x, y, z, 1 - c)
    to_x = {k: dev(xp(k), y, z, c) for k in (1, 3)}
    to_y = {k: dev(x, yp(k), z, c) for k in (1, 2, 3)}
    to_z = {k: dev(x, y, zp(k), c) for k in (1, 2, 3)}
    peers = [sib] + list(to_x.values()) + list(to_y.values()) + list(to_z.values())
    barrier = pltpu.get_barrier_semaphore()
    for peer in peers:
        pl.semaphore_signal(barrier, inc=1, device_id=peer, device_id_type=MESH)

    for w, ref in ((OUT, wo_ref), (VAL, wv_ref), (QRY, wq_ref), (KEY, wk_ref)):
        for u in range(2):
            wgt[u, w, z, y] = ref[:, u * 128 : u * 128 + 128]
    rel[zh] = jnp.zeros((8, 128), F32)
    rel[zh, 0:4, 0:32] = rb_ref[...]
    cot[x, c] = do_ref[...]

    net = Links(send_sem, recv_sem)

    def chunk(u, zz, yy, row, n):
        return wgt.at[u, pl.ds(0, 4), zz, yy, pl.ds(row, n)]

    def column(u, zz, row, n):
        return wgt.at[u, pl.ds(0, 4), zz, pl.ds(0, 4), pl.ds(row, n)]

    def line(u, yy, row, n):
        return wgt.at[u, pl.ds(0, 4), pl.ds(0, 4), yy, pl.ds(row, n)]

    def both_ways(name, src, to):
        net.start((name, 1), src, src, to[1])
        net.start((name, 3), src, src, to[3])

    def weights_a(u, hops):
        for k in hops:
            s = chunk(u, z, y, 0, 128)
            net.start(("y", u, k), s, s, to_y[k])
            s = chunk(u, z, y, 128, 128)
            net.start(("z", u, k), s, s, to_z[k])

    def weights_c(u):
        for k in (1, 3, 2):
            net.arrived("y", u, k)
        both_ways(("z2", u), column(u, z, 0, 128), to_z)
        for k in (1, 3, 2):
            net.arrived("z", u, k)
        both_ways(("y2", u), line(u, y, 128, 128), to_y)

    def weights_d(u):
        for k, row in ((1, 0), (3, 64)):
            net.arrived(("z2", u), k)
            s = column(u, zp(4 - k), row, 64)
            net.start(("z2f", u, k), s, s, to_z[k])
            net.arrived(("y2", u), k)
            s = line(u, yp(4 - k), 128 + row, 64)
            net.start(("y2f", u, k), s, s, to_y[k])

    def weights_here(u):
        for name in ("z2f", "y2f"):
            net.arrived(name, u, 1)
            net.arrived(name, u, 3)

    def tokens_a(name, buf):
        both_ways(name, buf.at[x, c], to_x)
        net.start((name, "sib", 0), buf.at[x, c], buf.at[x, c], sib)

    def tokens_b(name, buf):
        for k, row in ((1, 0), (3, 64)):
            net.arrived(name, k)
            s = buf.at[xp(4 - k), c, pl.ds(row, 64)]
            net.start((name, "f", k), s, s, to_x[k])
            s = buf.at[xp(4 - k), c]
            net.start((name, "sib", 4 - k), s, s, sib)

    def tokens_c(name, buf):
        net.arrived(name, "f", 1)
        net.arrived(name, "f", 3)
        s = buf.at[xp(2), c]
        net.start((name, "sib", 2), s, s, sib)

    def norm_rows(k):
        rows = x_ref[pl.ds(pl.multiple_of(k * 16, 16), 16), :].astype(F32)
        inv = lax.rsqrt(jnp.mean(rows * rows, axis=-1, keepdims=True) + EPSILON)
        return rows * inv, inv

    def normalize():
        @pl.loop(0, 8)
        def _(k):
            unit, _ = norm_rows(k)
            tok[x, c, pl.ds(pl.multiple_of(k * 16, 16), 16), :] = (unit * gain_ref[...]).astype(BF)

    def spread_bias():
        net.arrived("rel")
        steps = bucket_steps()
        table = jnp.concatenate([rel[0, 0:4, :], rel[1, 0:4, :]], axis=0)
        for k in range(BUCKETS):
            splat[k] = jnp.broadcast_to(table[:, k : k + 1], (8, 128))

        @pl.loop(0, LEN // 8)
        def _(k):
            i = lax.broadcasted_iota(jnp.int32, (8, LEN), 0) + k * 8
            r = lax.broadcasted_iota(jnp.int32, (8, LEN), 1) - i

            def row(b, h):
                return jnp.broadcast_to(splat[b, h : h + 1, 0:1], (8, LEN))

            values = [row(0, h) for h in range(8)]
            for b in range(1, BUCKETS // 2):
                for chosen, at in ((r <= -steps[b], b), (r >= steps[b], BUCKETS // 2 + b)):
                    for h in range(8):
                        values[h] = jnp.where(chosen, row(at, h), values[h])
            for h in range(8):
                bias[h, pl.ds(pl.multiple_of(k * 8, 8), 8), :] = values[h]

    lane = lax.broadcasted_iota(jnp.int32, (1, 128), 1)
    mask = [(lane < 64).astype(F32).astype(BF), (lane >= 64).astype(F32).astype(BF)]
    row_at = lax.broadcasted_iota(jnp.int32, (128, 1), 0)
    mask_t = [(row_at < 64).astype(F32).astype(BF), (row_at >= 64).astype(F32).astype(BF)]

    def passages(u, places):
        n = len(places)

        def by_chunk(buf):
            whole = jnp.concatenate([buf[p].reshape(256, 2048) for p in places], axis=0)
            order = [yy * 2 + zz for zz in range(2) for yy in range(4)]
            return jnp.concatenate([whole[:, i * 256 : i * 256 + 256] for i in order], axis=1)

        for w in range(4):
            left = by_chunk(cot if w == OUT else tok)
            right = jnp.concatenate([wgt[u, w, g * 2 : g * 2 + 2].reshape(2048, 128) for g in range(2)], axis=1)
            heads[w, 0 : n * 256] = dot_nn(left, right).astype(BF)
        for i, p in enumerate(places):
            attention(u, i, pl.ds(pl.multiple_of(p * 256, 256), 256))

    def attention(u, i, rows):
        parts = [
            tuple(heads[w, i * 256 : i * 256 + 256, g * 128 : g * 128 + 128] for w in range(4)) for g in range(2)
        ]
        scores = [
            [dot_nt(q2 * mask[h], k2) + bias[g * 4 + u * 2 + h] for h in range(2)]
            for g, (_, _, q2, k2) in enumerate(parts)
        ]
        d_prob = [[dot_nt(dc2 * mask[h], v2) for h in range(2)] for dc2, v2, _, _ in parts]
        probs_b, d_score = [[], []], [[], []]
        for g in range(2):
            for h in range(2):
                e = jnp.exp(scores[g][h] - jnp.max(scores[g][h], axis=-1, keepdims=True))
                probs = e * (1.0 / jnp.sum(e, axis=-1, keepdims=True))
                row_dot = jnp.sum(probs * d_prob[g][h], axis=-1, keepdims=True)
                probs_b[g].append(probs.astype(BF))
                d_score[g].append((probs * (d_prob[g][h] - row_dot)).astype(BF))
        for g, (dc2, v2, q2, k2) in enumerate(parts):
            ctx = dot_nn(
                jnp.concatenate(probs_b[g], axis=1),
                jnp.concatenate([v2 * mask[0], v2 * mask[1]], axis=0),
            ).astype(BF)
            dq = dot_nn(
                jnp.concatenate(d_score[g], axis=1),
                jnp.concatenate([k2 * mask[0], k2 * mask[1]], axis=0),
            ).astype(BF)
            dc_t, q_t = dc2.T, q2.T
            dv_t = dot_nn(
                jnp.concatenate([dc_t * mask_t[0], dc_t * mask_t[1]], axis=1),
                jnp.concatenate(probs_b[g], axis=0),
            ).astype(BF)
            dk_t = dot_nn(
                jnp.concatenate([q_t * mask_t[0], q_t * mask_t[1]], axis=1),
                jnp.concatenate(d_score[g], axis=0),
            ).astype(BF)
            at, lanes = pl.ds(g * 128, 128), pl.ds(g * 128, 128)
            rows_t[OUT, at, rows] = ctx.T
            rows_t[VAL, at, rows] = dv_t
            rows_t[QRY, at, rows] = dq.T
            rows_t[KEY, at, rows] = dk_t
            dheads[u, VAL - 1, rows, lanes] = dv_t.T
            dheads[u, QRY - 1, rows, lanes] = dq
            dheads[u, KEY - 1, rows, lanes] = dk_t.T

    def weight_grads(u, pair):
        if pair == 0:
            out = dot_nn(rows_t[OUT], cot[...].reshape(1024, 2048)).astype(BF)
            val = dot_nn(rows_t[VAL], tok[...].reshape(1024, 2048)).astype(BF)
            res = (out, val)
        else:
            both = dot_nn(rows_t[2:4].reshape(512, 1024), tok[...].reshape(1024, 2048)).astype(BF)
            res = (both[:256], both[256:])
        for w in range(2):
            for f in range(8):
                fy, fz = f // 2, f % 2
                for g in range(2):
                    for h in range(2):
                        at = g * 128 + h * 64
                        block = res[w][at : at + 64, f * 256 : f * 256 + 256]
                        if pair == 0:
                            part_y[u, fy, h, w, g, fz] = block
                        else:
                            part_z[u, g * 2 + fz, h, w, fy] = block

    def ring_far(key, block, far, near, to):
        net.start((key, "far", 1), block(2, 0), far(0), to[1])
        net.start((key, "far", 3), block(2, 1), far(1), to[3])

    def ring_near(k, key, block, far, near, to):
        half, side = (1, 0) if k == 1 else (0, 1)
        net.start((key, "near", k), block(k, half), near(side, half), to[k])

    def ring_both(k, add, key, block, far, near, to):
        half, side = (0, 0) if k == 1 else (1, 1)
        net.arrived(key, "far", k)
        add(block(k, half), far(side))
        net.start((key, "both", k), block(k, half), near(side, half), to[k])

    def ring_c(key):
        for k in (1, 3):
            net.arrived(key, "near", k)
            net.arrived(key, "both", k)

    def add_into(dst, src):
        dst[...] = (dst[...].astype(F32) + src[...].astype(F32)).astype(BF)

    def add_pair(dst, src):
        for w in range(2):
            add_into(dst.at[w], src.at[w])

    def first(u, pair):
        if pair == 0:
            return (
                ("s1", u, pair),
                lambda k, h: part_y.at[u, yp(k), h],
                lambda s: far_y.at[u, s],
                lambda s, h: near_y.at[u, s, h],
                to_y,
            )
        return (
            ("s1", u, pair),
            lambda k, h: part_z.at[u, zp(k), h],
            lambda s: far_z.at[u, s],
            lambda s, h: near_z.at[u, s, h],
            to_z,
        )

    def grads_a(u, pair):
        ring_far(*first(u, pair))
        for k in (1, 3):
            ring_near(k, *first(u, pair))

    def grads_b(u):
        for k in (1, 3):
            for pair in range(2):
                ring_both(k, add_pair, *first(u, pair))

    def grads_c(u):
        for pair in range(2):
            ring_c(first(u, pair)[0])
            own, near = (part_y.at[u, y], near_y.at[u]) if pair == 0 else (part_z.at[u, z], near_z.at[u])
            for h in range(2):
                for w in range(2):
                    total = own[h, w].astype(F32) + near[0, h, w].astype(F32) + near[1, h, w].astype(F32)
                    own[h, w] = total.astype(BF)
            for k in (2, 1, 3):
                if pair == 0:
                    src, to = part_y.at[u, y, pl.ds(0, 2), pl.ds(0, 2), zp(k) // 2, zp(k) % 2], to_z[k]
                else:
                    src, to = part_z.at[u, z, pl.ds(0, 2), pl.ds(0, 2), yp(k)], to_y[k]
                net.start(("s2", u, pair, k), src, last.at[u, pair, k - 1], to)

    def grads_e(u):
        for pair, outs in ((0, (go_ref, gv_ref)), (1, (gq_ref, gk_ref))):
            for k in (1, 3, 2):
                net.arrived("s2", u, pair, k)
            for w in range(2):
                for h in range(2):
                    own = part_y[u, y, h, w, zh, zl] if pair == 0 else part_z[u, z, h, w, y]
                    total = own.astype(F32)
                    for k in range(3):
                        total = total + last[u, pair, k, h, w].astype(F32)
                    outs[w][:, u * 128 + h * 64 : u * 128 + h * 64 + 64] = total.T

    def d_tokens(first, second):
        places = (xp(first), xp(second))
        pieces = [(u, w, g) for u in range(2) for w in range(3) for g in range(2)]
        left = jnp.concatenate(
            [
                jnp.concatenate(
                    [
                        dheads[u, w, pl.ds(pl.multiple_of(p * 256, 256), 256), g * 128 : g * 128 + 128]
                        for u, w, g in pieces
                    ],
                    axis=1,
                )
                for p in places
            ],
            axis=0,
        )
        for f in range(8):
            right = jnp.concatenate([wgt[u, w + 1, g * 2 + f % 2, f // 2] for u, w, g in pieces], axis=1)
            total = dot_nt(left, right).astype(BF)
            for i, p in enumerate(places):
                dn[p, :, :, f * 256 : f * 256 + 256] = total[i * 256 : i * 256 + 256].reshape(2, 128, 256)

    def d_cross(k):
        net.start(("dsib", k), dn.at[xp(k), 1 - c], dn_sib.at[xp(k)], sib)

    def add_rows(dst, src, n):
        @pl.loop(0, n // 16)
        def _(m):
            rows = pl.ds(pl.multiple_of(m * 16, 16), 16)
            dst[rows, :] = (dst[rows, :].astype(F32) + src[rows, :].astype(F32)).astype(BF)

    def d_merge(k):
        net.arrived("dsib", k)
        add_rows(dn.at[xp(k), c], dn_sib.at[xp(k)], 128)

    d_ring = (
        "dx",
        lambda k, h: dn.at[xp(k), c, pl.ds(h * 64, 64)],
        lambda s: far_x.at[s],
        lambda s, h: near_x.at[s, pl.ds(h * 64, 64)],
        to_x,
    )

    def d_inputs():
        ring_c(d_ring[0])

        @pl.loop(0, 8)
        def _(m):
            rows = pl.ds(pl.multiple_of(m * 16, 16), 16)
            unit, inv = norm_rows(m)
            d_normed = dn[x, c, rows, :].astype(F32) + near_x[0, rows, :].astype(F32) + near_x[1, rows, :].astype(F32)
            d_unit = d_normed * gain_ref[...]
            branch = inv * (d_unit - unit * jnp.mean(d_unit * unit, axis=-1, keepdims=True))
            dx_ref[rows, :] = (do_ref[rows, :].astype(F32) + branch).astype(BF)

    def d_add(dst, src):
        add_rows(dst, src, 64)

    normalize()
    pl.semaphore_wait(barrier, len(peers))
    weights_a(0, (2, 1, 3))
    tokens_a("cot", cot)
    tokens_a("tok", tok)
    net.start(("rel",), rel.at[zh], rel.at[zh], to_z[2])
    weights_a(1, (2,))
    weights_c(0)
    spread_bias()
    weights_a(1, (1, 3))
    tokens_b("cot", cot)
    weights_d(0)
    tokens_b("tok", tok)
    weights_here(0)
    weights_c(1)
    net.arrived("cot", "sib", 0)
    net.arrived("tok", "sib", 0)
    passages(0, [x])
    for name in ("cot", "tok"):
        net.arrived(name, "sib", 1)
        net.arrived(name, "sib", 3)
    tokens_c("cot", cot)
    passages(0, [xp(1), xp(3)])
    tokens_c("tok", tok)
    net.arrived("cot", "sib", 2)
    net.arrived("tok", "sib", 2)
    passages(0, [xp(2)])
    weight_grads(0, 0)
    weights_d(1)
    grads_a(0, 0)
    weight_grads(0, 1)
    grads_a(0, 1)
    weights_here(1)
    passages(1, [0, 1])
    grads_b(0)
    passages(1, [2, 3])
    weight_grads(1, 0)
    grads_a(1, 0)
    weight_grads(1, 1)
    grads_a(1, 1)
    grads_c(0)
    d_tokens(2, 1)
    d_cross(2)
    d_cross(1)
    d_merge(2)
    ring_far(*d_ring)
    d_merge(1)
    ring_near(1, *d_ring)
    grads_b(1)
    d_tokens(3, 0)
    d_cross(3)
    d_cross(0)
    ring_both(1, d_add, *d_ring)
    d_merge(3)
    ring_near(3, *d_ring)
    ring_both(3, d_add, *d_ring)
    grads_e(0)
    d_merge(0)
    grads_c(1)
    d_inputs()
    grads_e(1)
    net.finish()


def write_results(*refs):
    n = len(refs) // 2
    for src, dst in zip(refs[:n], refs[n:]):
        dst[...] = src[...]


def per_device(inputs, gain, w_query, w_key, w_value, w_out, rel_bias, d_output):
    vmem = pl.BlockSpec(memory_space=pltpu.VMEM)
    grad = jax.ShapeDtypeStruct((256, 256), F32)
    shapes = (jax.ShapeDtypeStruct((128, 2048), BF), grad, grad, grad, grad)
    results = pl.pallas_call(
        kernel,
        out_shape=shapes,
        in_specs=[vmem] * 8,
        out_specs=(vmem,) * 5,
        scratch_shapes=[
            pltpu.VMEM((4, 2, 128, 2048), BF),
            pltpu.VMEM((4, 2, 128, 2048), BF),
            pltpu.VMEM((2, 4, 4, 4, 256, 128), BF),
            pltpu.VMEM((2, 8, 128), F32),
            pltpu.VMEM((8, 256, 256), F32),
            pltpu.VMEM((4, 1024, 256), BF),
            pltpu.VMEM((2, 3, 1024, 256), BF),
            pltpu.VMEM((4, 256, 1024), BF),
            pltpu.VMEM((2, 4, 2, 2, 2, 2, 64, 256), BF),
            pltpu.VMEM((2, 4, 2, 2, 4, 64, 256), BF),
            pltpu.VMEM((2, 2, 2, 2, 2, 64, 256), BF),
            pltpu.VMEM((2, 2, 2, 4, 64, 256), BF),
            pltpu.VMEM((2, 2, 2, 2, 2, 2, 64, 256), BF),
            pltpu.VMEM((2, 2, 2, 2, 4, 64, 256), BF),
            pltpu.VMEM((2, 2, 3, 2, 2, 64, 256), BF),
            pltpu.VMEM((4, 2, 128, 2048), BF),
            pltpu.VMEM((4, 128, 2048), BF),
            pltpu.VMEM((2, 64, 2048), BF),
            pltpu.VMEM((2, 128, 2048), BF),
            pltpu.VMEM((32, 8, 128), F32),
            pltpu.SemaphoreType.DMA((N_COPIES,)),
            pltpu.SemaphoreType.DMA((N_COPIES,)),
        ],
        compiler_params=pltpu.CompilerParams(
            collective_id=0, has_side_effects=True, vmem_limit_bytes=62 * 1024 * 1024
        ),
        name="attention_backward",
    )(inputs, gain.reshape(1, -1), w_query, w_key, w_value, w_out, rel_bias, d_output)
    return pl.pallas_call(
        write_results,
        out_shape=shapes,
        in_specs=[vmem] * 5,
        out_specs=(vmem,) * 5,
        name="write_results",
    )(*results)


def solution(mesh):
    return jax.shard_map(
        per_device,
        mesh=mesh,
        in_specs=(
            P(("fsdp", "tensor"), None),
            P(),
            P("fsdp", "tensor"),
            P("fsdp", "tensor"),
            P("fsdp", "tensor"),
            P("fsdp", "tensor"),
            P("tensor", None),
            P(("fsdp", "tensor"), None),
        ),
        out_specs=(
            P(("fsdp", "tensor"), None),
            P("fsdp", "tensor"),
            P("fsdp", "tensor"),
            P("fsdp", "tensor"),
            P("fsdp", "tensor"),
        ),
        check_vma=False,
    )
```

time: 594 us -> 116 us (0.20)
  waiting for transfers between devices: 431 us -> 0 us
  Pallas kernels: 0 us -> 114 us
  matrix products: 85.2 us -> 0 us
  local copies, waits for them, and re-layouts: 37.5 us -> 0 us
  other arithmetic: 20 us -> 0 us
  between operations: 14.7 us -> 0.64 us
    all_gather x6 -> x0, waiting for transfers between devices: 270 us -> none  [the longest x1 75.6 us: per_device(): normed_all = lax.all_gather(normed, 'tensor', axis=0, tiled=True)]
    reduce_scatter x2 -> x0, waiting for transfers between devices: 158 us -> none  [the longest x1 103 us: per_device(): lax.psum_scatter(running.astype(jnp.bfloat16), 'tensor', scatter_dimensio...]
    pallas_call x0 -> x2, Pallas kernels: none -> 114 us  [the longest x1 112 us: per_device(): pl.pallas_call(kernel, out_shape=shapes, in_specs=[vmem] * 8, out_specs=(...]
    dot_general x16 -> x0, matrix products: 77.8 us -> none  [the longest x3 33.5 us: per_device(): jnp.einsum('te,de->td', gradient, weight, preferred_element_type=jnp.floa...]
    reshape x8 -> x0, local copies, waits for them, and re-layouts: 25.9 us -> none  [heads_view(): return array.reshape(rows_pass, length, local_heads, head_size)]
    sub x1 -> x0, matrix products: 7.48 us -> none  [per_device(): exp_scores = jnp.exp(scores - row_max)]
    add x1 -> x0, other arithmetic: 7.12 us -> none  [bias_grid(): expanded = expanded + rel_bias[:, bucket][:, None, None] * chosen[None]]
    unnamed x34 -> x0, local copies, waits for them, and re-layouts: 6.5 us -> none
  transfers between devices with their start and end apart: 8 -> 0, of which waited for: 8 -> 0; matrix products, arithmetic and copies ran while one was open for 13% -> 0% of each run, Pallas kernels for 0% -> 0%
where the time goes in v2:
time: 116 us; the launch traced here: 115 us
  Pallas kernels  114 us (98%)
    pallas_call x1, Pallas kernels, per_device(): pl.pallas_call(kernel, out_shape=shapes, in_specs=[vmem] * 8, out_specs=(...  112 us
    pallas_call x1, Pallas kernels, per_device(): pl.pallas_call(write_results, out_shape=shapes, in_specs=[vmem] * 5, out_...  2.5 us

profile of v2, /device:TPU:0, one launch (start us, length us, event | category | flops | bytes accessed | tf_op | source)
XLA Modules:
  0.0 115.0 jit_solution(5022152852856751165)
XLA Ops:
  0.6 111.8 %attention_backward.1 = (bf16[128,2048]{1,0:T(8,128)(2,1)}, f32[256,256]{1,0:T(8,128)}, f32[256,256]{1,0:T(8,128)}, f32[256,256]{1,0:T(8,128)}, f32[256,256]{1,0:T(8,128)}) custom-call(bf16[128,2048]{1,0:T(8,128)(2,1)} %x_ref.1, f32[1,2048]{1,0:T(1,128)} %bitcast.1, bf16[256,256]{1,0:T(8,128)(2,1)} %wq_ref.1, bf16[256,256]{1,0:T(8,128)(2,1)} %wk_ref.1, ...), custom_call_target="tpu_custom_call" | custom-call | tf_op jit(solution)/shard_map/attention_backward/pallas_call | solution.py:504
  112.5 2.5 %write_results.1 = (bf16[128,2048]{1,0:T(8,128)(2,1)}, f32[256,256]{1,0:T(8,128)}, f32[256,256]{1,0:T(8,128)}, f32[256,256]{1,0:T(8,128)}, f32[256,256]{1,0:T(8,128)}) custom-call(bf16[128,2048]{1,0:T(8,128)(2,1)} %get-tuple-element.10.refs_0_, f32[256,256]{1,0:T(8,128)} %get-tuple-element.11.refs_1_, f32[256,256]{1,0:T(8,128)} %get-tuple-element.12.refs_2_, ...), custom_call_target="tpu_custom_call" | custom-call | tf_op jit(solution)/shard_map/write_results/pallas_call | solution.py:538

commit v3 on v2

--- a/solution.py
+++ b/solution.py
@@ -42,39 +42,47 @@
 class Links:
     def __init__(self, send_sem, recv_sem):
         self.send_sem, self.recv_sem = send_sem, recv_sem
-        self.copies = {}
-
-    def start(self, key, src, dst, peer):
-        k = len(self.copies)
-        copy = pltpu.make_async_remote_copy(
+        self.groups = {}
+        self.sends = {}
+
+    def start(self, group, send, src, dst, peer):
+        k = self.groups.setdefault(group, len(self.groups))
+        j = self.sends.setdefault(send, len(self.sends))
+        pltpu.make_async_remote_copy(
             src_ref=src,
             dst_ref=dst,
-            send_sem=self.send_sem.at[k],
+            send_sem=self.send_sem.at[j],
+            recv_sem=self.recv_sem.at[k],
+            device_id=peer,
+            device_id_type=MESH,
+        ).start()
+
+    def waiter(self, j, k, ref, peer):
+        return pltpu.make_async_remote_copy(
+            src_ref=ref,
+            dst_ref=ref,
+            send_sem=self.send_sem.at[j],
             recv_sem=self.recv_sem.at[k],
             device_id=peer,
             device_id_type=MESH,
         )
-        copy.start()
-        assert key not in self.copies
-        self.copies[key] = copy
-
-    def arrived(self, *key):
-        self.copies[key].wait_recv()
-
-    def finish(self):
-        for copy in self.copies.values():
-            copy.wait_send()
-
-
-N_COPIES = 112
+
+    def arrived(self, group, ref, peer):
+        self.waiter(0, self.groups[group], ref, peer).wait_recv()
+
+    def sent(self, send, ref, peer):
+        self.waiter(self.sends[send], 0, ref, peer).wait_send()
+
+
+N_GROUPS, N_SENDS = 63, 6
 
 
 def kernel(
-    x_ref, gain_ref, wq_ref, wk_ref, wv_ref, wo_ref, rb_ref, do_ref,
+    x_in, gain_in, wq_in, wk_in, wv_in, wo_in, rb_in, do_in,
     dx_ref, gq_ref, gk_ref, gv_ref, go_ref,
     tok, cot, wgt, rel, bias, heads, dheads, rows_t,
-    part_y, part_z, far_y, far_z, near_y, near_z, last,
-    dn, dn_sib, far_x, near_x, splat, send_sem, recv_sem,
+    part_y, part_z, far_y, far_z, near_y, near_z, far2, near2,
+    dn, dn_sib, far_x, near_x, splat, x_ref, gain_ref, rb_ref, send_sem, recv_sem, load_sem,
 ):
     f, t = lax.axis_index("fsdp"), lax.axis_index("tensor")
     x, zh, c = t // 4, (t // 2) % 2, t % 2
@@ -102,12 +110,15 @@
     for peer in peers:
         pl.semaphore_signal(barrier, inc=1, device_id=peer, device_id_type=MESH)
 
-    for w, ref in ((OUT, wo_ref), (VAL, wv_ref), (QRY, wq_ref), (KEY, wk_ref)):
-        for u in range(2):
-            wgt[u, w, z, y] = ref[:, u * 128 : u * 128 + 128]
-    rel[zh] = jnp.zeros((8, 128), F32)
-    rel[zh, 0:4, 0:32] = rb_ref[...]
-    cot[x, c] = do_ref[...]
+    loads = [(x_in, x_ref, 0), (gain_in, gain_ref, 1), (rb_in, rb_ref, 2), (do_in, cot.at[x, c], 3)]
+    for u in range(2):
+        for w, ref in ((OUT, wo_in), (VAL, wv_in), (QRY, wq_in), (KEY, wk_in)):
+            loads.append((ref.at[:, pl.ds(u * 128, 128)], wgt.at[u, w, z, y], 4))
+    for src, dst, i in loads:
+        pltpu.make_async_copy(src, dst, load_sem.at[i]).start()
+
+    def loaded(i, ref):
+        pltpu.make_async_copy(ref, ref, load_sem.at[i]).wait()
 
     net = Links(send_sem, recv_sem)
 
@@ -120,56 +131,66 @@
     def line(u, yy, row, n):
         return wgt.at[u, pl.ds(0, 4), pl.ds(0, 4), yy, pl.ds(row, n)]
 
-    def both_ways(name, src, to):
-        net.start((name, 1), src, src, to[1])
-        net.start((name, 3), src, src, to[3])
-
-    def weights_a(u, hops):
-        for k in hops:
-            s = chunk(u, z, y, 0, 128)
-            net.start(("y", u, k), s, s, to_y[k])
-            s = chunk(u, z, y, 128, 128)
-            net.start(("z", u, k), s, s, to_z[k])
+    def arrived(group, ref):
+        net.arrived(group, ref, sib)
+
+    def weights_a(u):
+        for part in range(2):
+            for k, row in ((1, part * 64), (3, 64 - part * 64)):
+                for name, to, at in (("y", to_y, 0), ("z", to_z, 128)):
+                    s = chunk(u, z, y, at + row, 64)
+                    net.start((name, u) if part else (name, u, k), "w", s, s, to[k])
+
+    def weights_b(u):
+        for k, row in ((1, 0), (3, 64)):
+            s = chunk(u, z, yp(4 - k), row, 64)
+            arrived(("y", u, k), s)
+            net.start(("y", u), "w", s, s, to_y[k])
+            s = chunk(u, zp(4 - k), y, 128 + row, 64)
+            arrived(("z", u, k), s)
+            net.start(("z", u), "w", s, s, to_z[k])
 
     def weights_c(u):
-        for k in (1, 3, 2):
-            net.arrived("y", u, k)
-        both_ways(("z2", u), column(u, z, 0, 128), to_z)
-        for k in (1, 3, 2):
-            net.arrived("z", u, k)
-        both_ways(("y2", u), line(u, y, 128, 128), to_y)
+        arrived(("y", u), column(u, z, 0, 64))
+        for part in range(2):
+            for k, row in ((1, part * 64), (3, 64 - part * 64)):
+                s = column(u, z, row, 64)
+                net.start(("all", u) if part else ("z2", u, k), "w", s, s, to_z[k])
+        arrived(("z", u), line(u, y, 128, 64))
+        for part in range(2):
+            for k, row in ((1, part * 64), (3, 64 - part * 64)):
+                s = line(u, y, 128 + row, 64)
+                net.start(("all", u) if part else ("y2", u, k), "w", s, s, to_y[k])
 
     def weights_d(u):
         for k, row in ((1, 0), (3, 64)):
-            net.arrived(("z2", u), k)
             s = column(u, zp(4 - k), row, 64)
-            net.start(("z2f", u, k), s, s, to_z[k])
-            net.arrived(("y2", u), k)
+            arrived(("z2", u, k), s)
+            net.start(("all", u), "w", s, s, to_z[k])
             s = line(u, yp(4 - k), 128 + row, 64)
-            net.start(("y2f", u, k), s, s, to_y[k])
+            arrived(("y2", u, k), s)
+            net.start(("all", u), "w", s, s, to_y[k])
 
     def weights_here(u):
-        for name in ("z2f", "y2f"):
-            net.arrived(name, u, 1)
-            net.arrived(name, u, 3)
+        arrived(("all", u), wgt.at[u, pl.ds(0, 4), pl.ds(0, 4), pl.ds(0, 4), pl.ds(0, 128)])
 
     def tokens_a(name, buf):
-        both_ways(name, buf.at[x, c], to_x)
-        net.start((name, "sib", 0), buf.at[x, c], buf.at[x, c], sib)
+        for k in (1, 3):
+            net.start((name, k), name, buf.at[x, c], buf.at[x, c], to_x[k])
+        net.start("own", name, buf.at[x, c], buf.at[x, c], sib)
 
     def tokens_b(name, buf):
         for k, row in ((1, 0), (3, 64)):
-            net.arrived(name, k)
+            arrived((name, k), buf.at[xp(4 - k), c])
             s = buf.at[xp(4 - k), c, pl.ds(row, 64)]
-            net.start((name, "f", k), s, s, to_x[k])
+            net.start((name, "far"), name, s, s, to_x[k])
             s = buf.at[xp(4 - k), c]
-            net.start((name, "sib", 4 - k), s, s, sib)
+            net.start("near", name, s, s, sib)
 
     def tokens_c(name, buf):
-        net.arrived(name, "f", 1)
-        net.arrived(name, "f", 3)
         s = buf.at[xp(2), c]
-        net.start((name, "sib", 2), s, s, sib)
+        arrived((name, "far"), s)
+        net.start("far", name, s, s, sib)
 
     def norm_rows(k):
         rows = x_ref[pl.ds(pl.multiple_of(k * 16, 16), 16), :].astype(F32)
@@ -183,7 +204,7 @@
             tok[x, c, pl.ds(pl.multiple_of(k * 16, 16), 16), :] = (unit * gain_ref[...]).astype(BF)
 
     def spread_bias():
-        net.arrived("rel")
+        arrived("rel", rel.at[zh])
         steps = bucket_steps()
         table = jnp.concatenate([rel[0, 0:4, :], rel[1, 0:4, :]], axis=0)
         for k in range(BUCKETS):
@@ -289,24 +310,19 @@
                         else:
                             part_z[u, g * 2 + fz, h, w, fy] = block
 
-    def ring_far(key, block, far, near, to):
-        net.start((key, "far", 1), block(2, 0), far(0), to[1])
-        net.start((key, "far", 3), block(2, 1), far(1), to[3])
-
-    def ring_near(k, key, block, far, near, to):
+    def ring_far(key, block, far, near, to, send):
+        net.start((key, 1), send, block(2, 0), far(0), to[1])
+        net.start((key, 3), send, block(2, 1), far(1), to[3])
+
+    def ring_near(k, key, block, far, near, to, send):
         half, side = (1, 0) if k == 1 else (0, 1)
-        net.start((key, "near", k), block(k, half), near(side, half), to[k])
-
-    def ring_both(k, add, key, block, far, near, to):
+        net.start(key, send, block(k, half), near(side, half), to[k])
+
+    def ring_both(k, add, key, block, far, near, to, send):
         half, side = (0, 0) if k == 1 else (1, 1)
-        net.arrived(key, "far", k)
+        arrived((key, k), far(side))
         add(block(k, half), far(side))
-        net.start((key, "both", k), block(k, half), near(side, half), to[k])
-
-    def ring_c(key):
-        for k in (1, 3):
-            net.arrived(key, "near", k)
-            net.arrived(key, "both", k)
+        net.start(key, send, block(k, half), near(side, half), to[k])
 
     def add_into(dst, src):
         dst[...] = (dst[...].astype(F32) + src[...].astype(F32)).astype(BF)
@@ -323,6 +339,7 @@
                 lambda s: far_y.at[u, s],
                 lambda s, h: near_y.at[u, s, h],
                 to_y,
+                "sums",
             )
         return (
             ("s1", u, pair),
@@ -330,6 +347,22 @@
             lambda s: far_z.at[u, s],
             lambda s, h: near_z.at[u, s, h],
             to_z,
+            "sums",
+        )
+
+    def second(u, pair):
+        def block(k, h):
+            if pair == 0:
+                return part_y.at[u, y, h, pl.ds(0, 2), zp(k) // 2, zp(k) % 2]
+            return part_z.at[u, z, h, pl.ds(0, 2), yp(k)]
+
+        return (
+            ("s2", u, pair),
+            block,
+            lambda s: far2.at[u, pair, s],
+            lambda s, h: near2.at[u, pair, s, h],
+            to_z if pair == 0 else to_y,
+            "sums",
         )
 
     def grads_a(u, pair):
@@ -344,55 +377,55 @@
 
     def grads_c(u):
         for pair in range(2):
-            ring_c(first(u, pair)[0])
             own, near = (part_y.at[u, y], near_y.at[u]) if pair == 0 else (part_z.at[u, z], near_z.at[u])
+            arrived(("s1", u, pair), near)
             for h in range(2):
                 for w in range(2):
                     total = own[h, w].astype(F32) + near[0, h, w].astype(F32) + near[1, h, w].astype(F32)
                     own[h, w] = total.astype(BF)
-            for k in (2, 1, 3):
-                if pair == 0:
-                    src, to = part_y.at[u, y, pl.ds(0, 2), pl.ds(0, 2), zp(k) // 2, zp(k) % 2], to_z[k]
-                else:
-                    src, to = part_z.at[u, z, pl.ds(0, 2), pl.ds(0, 2), yp(k)], to_y[k]
-                net.start(("s2", u, pair, k), src, last.at[u, pair, k - 1], to)
+            ring_far(*second(u, pair))
+
+    def grads_near(u):
+        for pair in range(2):
+            for k in (1, 3):
+                ring_near(k, *second(u, pair))
+
+    def grads_d(u):
+        for k in (1, 3):
+            for pair in range(2):
+                ring_both(k, add_into, *second(u, pair))
 
     def grads_e(u):
         for pair, outs in ((0, (go_ref, gv_ref)), (1, (gq_ref, gk_ref))):
-            for k in (1, 3, 2):
-                net.arrived("s2", u, pair, k)
+            near = near2.at[u, pair]
+            arrived(("s2", u, pair), near)
             for w in range(2):
                 for h in range(2):
                     own = part_y[u, y, h, w, zh, zl] if pair == 0 else part_z[u, z, h, w, y]
-                    total = own.astype(F32)
-                    for k in range(3):
-                        total = total + last[u, pair, k, h, w].astype(F32)
+                    total = own.astype(F32) + near[0, h, w].astype(F32) + near[1, h, w].astype(F32)
                     outs[w][:, u * 128 + h * 64 : u * 128 + h * 64 + 64] = total.T
 
-    def d_tokens(first, second):
-        places = (xp(first), xp(second))
-        pieces = [(u, w, g) for u in range(2) for w in range(3) for g in range(2)]
+    def d_tokens(u, places):
+        pieces = [(w, g) for w in range(3) for g in range(2)]
         left = jnp.concatenate(
             [
-                jnp.concatenate(
-                    [
-                        dheads[u, w, pl.ds(pl.multiple_of(p * 256, 256), 256), g * 128 : g * 128 + 128]
-                        for u, w, g in pieces
-                    ],
-                    axis=1,
-                )
+                jnp.concatenate([dheads[u, w, pl.ds(pl.multiple_of(p * 256, 256), 256), :] for w in range(3)], axis=1)
                 for p in places
             ],
             axis=0,
         )
         for f in range(8):
-            right = jnp.concatenate([wgt[u, w + 1, g * 2 + f % 2, f // 2] for u, w, g in pieces], axis=1)
-            total = dot_nt(left, right).astype(BF)
+            cols = pl.ds(f * 256, 256)
+            right = jnp.concatenate([wgt[u, w + 1, g * 2 + f % 2, f // 2] for w, g in pieces], axis=1)
+            total = dot_nt(left, right)
             for i, p in enumerate(places):
-                dn[p, :, :, f * 256 : f * 256 + 256] = total[i * 256 : i * 256 + 256].reshape(2, 128, 256)
+                block = total[i * 256 : i * 256 + 256].reshape(2, 128, 256)
+                if u:
+                    block = block + dn[p, :, :, cols].astype(F32)
+                dn[p, :, :, cols] = block.astype(BF)
 
     def d_cross(k):
-        net.start(("dsib", k), dn.at[xp(k), 1 - c], dn_sib.at[xp(k)], sib)
+        net.start(("cross", k), "dn", dn.at[xp(k), 1 - c], dn_sib.at[xp(k)], sib)
 
     def add_rows(dst, src, n):
         @pl.loop(0, n // 16)
@@ -401,7 +434,7 @@
             dst[rows, :] = (dst[rows, :].astype(F32) + src[rows, :].astype(F32)).astype(BF)
 
     def d_merge(k):
-        net.arrived("dsib", k)
+        arrived(("cross", k), dn_sib.at[xp(k)])
         add_rows(dn.at[xp(k), c], dn_sib.at[xp(k)], 128)
 
     d_ring = (
@@ -410,10 +443,11 @@
         lambda s: far_x.at[s],
         lambda s, h: near_x.at[s, pl.ds(h * 64, 64)],
         to_x,
+        "dn",
     )
 
     def d_inputs():
-        ring_c(d_ring[0])
+        arrived("dx", near_x)
 
         @pl.loop(0, 8)
         def _(m):
@@ -422,43 +456,48 @@
             d_normed = dn[x, c, rows, :].astype(F32) + near_x[0, rows, :].astype(F32) + near_x[1, rows, :].astype(F32)
             d_unit = d_normed * gain_ref[...]
             branch = inv * (d_unit - unit * jnp.mean(d_unit * unit, axis=-1, keepdims=True))
-            dx_ref[rows, :] = (do_ref[rows, :].astype(F32) + branch).astype(BF)
+            dx_ref[rows, :] = (cot[x, c, rows, :].astype(F32) + branch).astype(BF)
 
     def d_add(dst, src):
         add_rows(dst, src, 64)
 
+    loaded(2, rb_ref)
+    rel[zh] = jnp.zeros((8, 128), F32)
+    rel[zh, 0:4, 0:32] = rb_ref[...]
+    loaded(0, x_ref)
+    loaded(1, gain_ref)
     normalize()
+    loaded(3, cot.at[x, c])
+    loaded(4, wgt.at[pl.ds(0, 2), pl.ds(0, 4), z, y])
     pl.semaphore_wait(barrier, len(peers))
-    weights_a(0, (2, 1, 3))
+    weights_a(0)
     tokens_a("cot", cot)
     tokens_a("tok", tok)
-    net.start(("rel",), rel.at[zh], rel.at[zh], to_z[2])
-    weights_a(1, (2,))
+    net.start("rel", "rel", rel.at[zh], rel.at[zh], to_z[2])
+    weights_b(0)
+    weights_a(1)
     weights_c(0)
+    weights_b(1)
     spread_bias()
-    weights_a(1, (1, 3))
+    weights_d(0)
     tokens_b("cot", cot)
-    weights_d(0)
+    weights_c(1)
     tokens_b("tok", tok)
     weights_here(0)
-    weights_c(1)
-    net.arrived("cot", "sib", 0)
-    net.arrived("tok", "sib", 0)
+    arrived("own", tok.at[pl.ds(0, 2), 0])
     passages(0, [x])
-    for name in ("cot", "tok"):
-        net.arrived(name, "sib", 1)
-        net.arrived(name, "sib", 3)
+    arrived("near", tok.at[pl.ds(0, 4), 0])
     tokens_c("cot", cot)
     passages(0, [xp(1), xp(3)])
+    weights_d(1)
     tokens_c("tok", tok)
-    net.arrived("cot", "sib", 2)
-    net.arrived("tok", "sib", 2)
+    arrived("far", tok.at[pl.ds(0, 2), 0])
     passages(0, [xp(2)])
     weight_grads(0, 0)
-    weights_d(1)
     grads_a(0, 0)
     weight_grads(0, 1)
     grads_a(0, 1)
+    d_tokens(0, [0, 1, 2, 3])
     weights_here(1)
     passages(1, [0, 1])
     grads_b(0)
@@ -467,44 +506,55 @@
     grads_a(1, 0)
     weight_grads(1, 1)
     grads_a(1, 1)
-    grads_c(0)
-    d_tokens(2, 1)
+    d_tokens(1, [xp(2), xp(1)])
     d_cross(2)
     d_cross(1)
+    grads_c(0)
+    d_tokens(1, [xp(3), x])
+    d_cross(3)
+    d_cross(0)
     d_merge(2)
     ring_far(*d_ring)
     d_merge(1)
     ring_near(1, *d_ring)
     grads_b(1)
-    d_tokens(3, 0)
-    d_cross(3)
-    d_cross(0)
-    ring_both(1, d_add, *d_ring)
+    grads_near(0)
     d_merge(3)
     ring_near(3, *d_ring)
+    d_merge(0)
+    ring_both(1, d_add, *d_ring)
     ring_both(3, d_add, *d_ring)
+    grads_d(0)
+    grads_c(1)
+    grads_near(1)
     grads_e(0)
-    d_merge(0)
-    grads_c(1)
+    grads_d(1)
     d_inputs()
     grads_e(1)
-    net.finish()
+    w_all = wgt.at[pl.ds(0, 2), pl.ds(0, 4), pl.ds(0, 4), pl.ds(0, 4), pl.ds(0, 240)]
+    rows_all = tok.at[pl.ds(0, 4), pl.ds(0, 2), pl.ds(0, 112)]
+    sizes = {"w": w_all, "cot": rows_all, "tok": rows_all, "rel": rel.at[zh], "sums": w_all, "dn": rows_all}
+    for name, ref in sizes.items():
+        net.sent(name, ref, sib)
 
 
 def write_results(*refs):
     n = len(refs) // 2
-    for src, dst in zip(refs[:n], refs[n:]):
-        dst[...] = src[...]
+    copies = [pltpu.make_async_copy(refs[i], refs[n + i], refs[-1].at[i]) for i in range(n)]
+    for copy in copies:
+        copy.start()
+    for copy in copies:
+        copy.wait()
 
 
 def per_device(inputs, gain, w_query, w_key, w_value, w_out, rel_bias, d_output):
-    vmem = pl.BlockSpec(memory_space=pltpu.VMEM)
+    vmem, anywhere = pl.BlockSpec(memory_space=pltpu.VMEM), pl.BlockSpec(memory_space=pl.ANY)
     grad = jax.ShapeDtypeStruct((256, 256), F32)
     shapes = (jax.ShapeDtypeStruct((128, 2048), BF), grad, grad, grad, grad)
     results = pl.pallas_call(
         kernel,
-        out_shape=shapes,
-        in_specs=[vmem] * 8,
+        out_shape=tuple(pltpu.VMEM(s.shape, s.dtype) for s in shapes),
+        in_specs=[anywhere] * 8,
         out_specs=(vmem,) * 5,
         scratch_shapes=[
             pltpu.VMEM((4, 2, 128, 2048), BF),
@@ -521,17 +571,22 @@
             pltpu.VMEM((2, 2, 2, 4, 64, 256), BF),
             pltpu.VMEM((2, 2, 2, 2, 2, 2, 64, 256), BF),
             pltpu.VMEM((2, 2, 2, 2, 4, 64, 256), BF),
-            pltpu.VMEM((2, 2, 3, 2, 2, 64, 256), BF),
+            pltpu.VMEM((2, 2, 2, 2, 64, 256), BF),
+            pltpu.VMEM((2, 2, 2, 2, 2, 64, 256), BF),
             pltpu.VMEM((4, 2, 128, 2048), BF),
             pltpu.VMEM((4, 128, 2048), BF),
             pltpu.VMEM((2, 64, 2048), BF),
             pltpu.VMEM((2, 128, 2048), BF),
             pltpu.VMEM((32, 8, 128), F32),
-            pltpu.SemaphoreType.DMA((N_COPIES,)),
-            pltpu.SemaphoreType.DMA((N_COPIES,)),
+            pltpu.VMEM((128, 2048), BF),
+            pltpu.VMEM((1, 2048), F32),
+            pltpu.VMEM((4, 32), F32),
+            pltpu.SemaphoreType.DMA((N_SENDS,)),
+            pltpu.SemaphoreType.DMA((N_GROUPS,)),
+            pltpu.SemaphoreType.DMA((5,)),
         ],
         compiler_params=pltpu.CompilerParams(
-            collective_id=0, has_side_effects=True, vmem_limit_bytes=62 * 1024 * 1024
+            collective_id=0, has_side_effects=True, vmem_limit_bytes=60 * 1024 * 1024
         ),
         name="attention_backward",
     )(inputs, gain.reshape(1, -1), w_query, w_key, w_value, w_out, rel_bias, d_output)
@@ -539,7 +594,9 @@
         write_results,
         out_shape=shapes,
         in_specs=[vmem] * 5,
-        out_specs=(vmem,) * 5,
+        out_specs=(anywhere,) * 5,
+        scratch_shapes=[pltpu.SemaphoreType.DMA((5,))],
+        compiler_params=pltpu.CompilerParams(vmem_limit_bytes=8 * 1024 * 1024),
         name="write_results",
     )(*results)
 

time: 116 us -> 102 us (0.88)
  Pallas kernels: 114 us -> 99.4 us
    pallas_call x1, Pallas kernels: 112 us -> 98.2 us  [per_device(): pl.pallas_call(kernel, out_shape=tuple((pltpu.VMEM(s.shape, s.dtype) for...]
    pallas_call x1, Pallas kernels: 2.5 us -> 1.18 us  [per_device(): pl.pallas_call(write_results, out_shape=shapes, in_specs=[vmem] * 5, out_...]
where the time goes in v3:
time: 102 us; the launch traced here: 100 us
  Pallas kernels  99.4 us (97%)
    pallas_call x1, Pallas kernels, per_device(): pl.pallas_call(kernel, out_shape=tuple((pltpu.VMEM(s.shape, s.dtype) for...  98.2 us

profile of v3, /device:TPU:0, one launch (start us, length us, event | category | flops | bytes accessed | tf_op | source)
XLA Modules:
  0.0 100.2 jit_solution(9244213903742040695)
XLA Ops:
  0.6 98.2 %attention_backward.1 = (bf16[128,2048]{1,0:T(8,128)(2,1)S(1)}, f32[256,256]{1,0:T(8,128)S(1)}, f32[256,256]{1,0:T(8,128)S(1)}, f32[256,256]{1,0:T(8,128)S(1)}, f32[256,256]{1,0:T(8,128)S(1)}) custom-call(bf16[128,2048]{1,0:T(8,128)(2,1)} %x_in.1, f32[1,2048]{1,0:T(1,128)} %bitcast.1, bf16[256,256]{1,0:T(8,128)(2,1)} %wq_in.1, bf16[256,256]{1,0:T(8,128)(2,1)} %wk_in.1, ...), custom_call_target="tpu_custom_call" | custom-call | tf_op jit(solution)/shard_map/attention_backward/pallas_call | solution.py:554
  98.8 1.2 %write_results.1 = (bf16[128,2048]{1,0:T(8,128)(2,1)}, f32[256,256]{1,0:T(8,128)}, f32[256,256]{1,0:T(8,128)}, f32[256,256]{1,0:T(8,128)}, f32[256,256]{1,0:T(8,128)}) custom-call(bf16[128,2048]{1,0:T(8,128)(2,1)S(1)} %get-tuple-element.10.refs_0_, f32[256,256]{1,0:T(8,128)S(1)} %get-tuple-element.11.refs_1_, f32[256,256]{1,0:T(8,128)S(1)} %get-tuple-element.12.refs_2_, ...), custom_call_target="tpu_custom_call" | custom-call | tf_op jit(solution)/shard_map/write_results/pallas_call | solution.py:593

commit v4 on v3

--- a/solution.py
+++ b/solution.py
@@ -103,7 +103,7 @@
 
     sib = dev(x, y, z, 1 - c)
     to_x = {k: dev(xp(k), y, z, c) for k in (1, 3)}
-    to_y = {k: dev(x, yp(k), z, c) for k in (1, 2, 3)}
+    to_y = {k: dev(x, yp(k), z, c) for k in (1, 3)}
     to_z = {k: dev(x, y, zp(k), c) for k in (1, 2, 3)}
     peers = [sib] + list(to_x.values()) + list(to_y.values()) + list(to_z.values())
     barrier = pltpu.get_barrier_semaphore()
@@ -282,33 +282,33 @@
                 jnp.concatenate(d_score[g], axis=0),
             ).astype(BF)
             at, lanes = pl.ds(g * 128, 128), pl.ds(g * 128, 128)
-            rows_t[OUT, at, rows] = ctx.T
-            rows_t[VAL, at, rows] = dv_t
-            rows_t[QRY, at, rows] = dq.T
-            rows_t[KEY, at, rows] = dk_t
+            rows_t[u, OUT, at, rows] = ctx.T
+            rows_t[u, VAL, at, rows] = dv_t
+            rows_t[u, QRY, at, rows] = dq.T
+            rows_t[u, KEY, at, rows] = dk_t
             dheads[u, VAL - 1, rows, lanes] = dv_t.T
             dheads[u, QRY - 1, rows, lanes] = dq
             dheads[u, KEY - 1, rows, lanes] = dk_t.T
 
-    def weight_grads(u, pair):
-        if pair == 0:
-            out = dot_nn(rows_t[OUT], cot[...].reshape(1024, 2048)).astype(BF)
-            val = dot_nn(rows_t[VAL], tok[...].reshape(1024, 2048)).astype(BF)
-            res = (out, val)
-        else:
-            both = dot_nn(rows_t[2:4].reshape(512, 1024), tok[...].reshape(1024, 2048)).astype(BF)
-            res = (both[:256], both[256:])
+    def weight_grads(u, k):
+        cols = pl.ds(pl.multiple_of(yp(k) * 512, 512), 512)
+        for w, buf in ((OUT, cot), (VAL, tok)):
+            res = dot_nn(rows_t[u, w], buf[:, :, :, cols].reshape(1024, 512)).astype(BF)
+            for g in range(2):
+                for h in range(2):
+                    at = g * 128 + h * 64
+                    for fz in range(2):
+                        part_y[u, yp(k), h, w, g, fz] = res[at : at + 64, fz * 256 : fz * 256 + 256]
+        rows = pl.ds(pl.multiple_of(zp(k) // 2 * 128, 128), 128)
+        left = jnp.concatenate([rows_t[u, w, rows] for w in (QRY, KEY)], axis=0)
+        starts = [pl.multiple_of((fy * 2 + zp(k) % 2) * 256, 256) for fy in range(4)]
+        right = jnp.concatenate([tok[:, :, :, pl.ds(at, 256)].reshape(1024, 256) for at in starts], axis=1)
+        res = dot_nn(left, right).astype(BF)
         for w in range(2):
-            for f in range(8):
-                fy, fz = f // 2, f % 2
-                for g in range(2):
-                    for h in range(2):
-                        at = g * 128 + h * 64
-                        block = res[w][at : at + 64, f * 256 : f * 256 + 256]
-                        if pair == 0:
-                            part_y[u, fy, h, w, g, fz] = block
-                        else:
-                            part_z[u, g * 2 + fz, h, w, fy] = block
+            for h in range(2):
+                at = w * 128 + h * 64
+                for fy in range(4):
+                    part_z[u, zp(k), h, w, fy] = res[at : at + 64, fy * 256 : fy * 256 + 256]
 
     def ring_far(key, block, far, near, to, send):
         net.start((key, 1), send, block(2, 0), far(0), to[1])
@@ -365,9 +365,12 @@
             "sums",
         )
 
-    def grads_a(u, pair):
-        ring_far(*first(u, pair))
-        for k in (1, 3):
+    def grads_far(u):
+        for pair in range(2):
+            ring_far(*first(u, pair))
+
+    def grads_next(u, k):
+        for pair in range(2):
             ring_near(k, *first(u, pair))
 
     def grads_b(u):
@@ -488,43 +491,50 @@
     passages(0, [x])
     arrived("near", tok.at[pl.ds(0, 4), 0])
     tokens_c("cot", cot)
-    passages(0, [xp(1), xp(3)])
+    passages(0, [xp(1)])
     weights_d(1)
     tokens_c("tok", tok)
+    passages(0, [xp(3)])
     arrived("far", tok.at[pl.ds(0, 2), 0])
     passages(0, [xp(2)])
-    weight_grads(0, 0)
-    grads_a(0, 0)
-    weight_grads(0, 1)
-    grads_a(0, 1)
-    d_tokens(0, [0, 1, 2, 3])
+    weight_grads(0, 2)
+    grads_far(0)
+    for k in (1, 3):
+        weight_grads(0, k)
+        grads_next(0, k)
+    d_tokens(0, [xp(2), xp(1), xp(3)])
     weights_here(1)
     passages(1, [0, 1])
     grads_b(0)
     passages(1, [2, 3])
-    weight_grads(1, 0)
-    grads_a(1, 0)
-    weight_grads(1, 1)
-    grads_a(1, 1)
-    d_tokens(1, [xp(2), xp(1)])
+    weight_grads(1, 2)
+    grads_far(1)
+    d_tokens(1, [xp(2)])
     d_cross(2)
-    d_cross(1)
-    grads_c(0)
-    d_tokens(1, [xp(3), x])
-    d_cross(3)
-    d_cross(0)
+    for k in (1, 3):
+        weight_grads(1, k)
+        grads_next(1, k)
     d_merge(2)
     ring_far(*d_ring)
+    d_tokens(1, [xp(1), xp(3)])
+    d_cross(1)
+    d_cross(3)
+    weight_grads(0, 0)
     d_merge(1)
     ring_near(1, *d_ring)
+    d_merge(3)
+    ring_near(3, *d_ring)
+    grads_c(0)
     grads_b(1)
     grads_near(0)
-    d_merge(3)
-    ring_near(3, *d_ring)
-    d_merge(0)
+    weight_grads(1, 0)
     ring_both(1, d_add, *d_ring)
     ring_both(3, d_add, *d_ring)
+    d_tokens(0, [x])
+    d_tokens(1, [x])
+    d_cross(0)
     grads_d(0)
+    d_merge(0)
     grads_c(1)
     grads_near(1)
     grads_e(0)
@@ -564,7 +574,7 @@
             pltpu.VMEM((8, 256, 256), F32),
             pltpu.VMEM((4, 1024, 256), BF),
             pltpu.VMEM((2, 3, 1024, 256), BF),
-            pltpu.VMEM((4, 256, 1024), BF),
+            pltpu.VMEM((2, 4, 256, 1024), BF),
             pltpu.VMEM((2, 4, 2, 2, 2, 2, 64, 256), BF),
             pltpu.VMEM((2, 4, 2, 2, 4, 64, 256), BF),
             pltpu.VMEM((2, 2, 2, 2, 2, 64, 256), BF),

time: 102 us -> 98.5 us (0.966); the launches traced: 100 us -> 98.3 us
  Pallas kernels: 99.4 us -> 97.4 us
    pallas_call x1, Pallas kernels: 98.2 us -> 96.3 us  [per_device(): pl.pallas_call(kernel, out_shape=tuple((pltpu.VMEM(s.shape, s.dtype) for...]
where the time goes in v4:
time: 98.5 us; the launch traced here: 98.3 us
  Pallas kernels  97.4 us (99%)
    pallas_call x1, Pallas kernels, per_device(): pl.pallas_call(kernel, out_shape=tuple((pltpu.VMEM(s.shape, s.dtype) for...  96.3 us

profile of v4, /device:TPU:0, one launch (start us, length us, event | category | flops | bytes accessed | tf_op | source)
XLA Modules:
  0.0 98.3 jit_solution(17131270785875014073)
XLA Ops:
  0.6 96.3 %attention_backward.1 = (bf16[128,2048]{1,0:T(8,128)(2,1)S(1)}, f32[256,256]{1,0:T(8,128)S(1)}, f32[256,256]{1,0:T(8,128)S(1)}, f32[256,256]{1,0:T(8,128)S(1)}, f32[256,256]{1,0:T(8,128)S(1)}) custom-call(bf16[128,2048]{1,0:T(8,128)(2,1)} %x_in.1, f32[1,2048]{1,0:T(1,128)} %bitcast.1, bf16[256,256]{1,0:T(8,128)(2,1)} %wq_in.1, bf16[256,256]{1,0:T(8,128)(2,1)} %wk_in.1, ...), custom_call_target="tpu_custom_call" | custom-call | tf_op jit(solution)/shard_map/attention_backward/pallas_call | solution.py:564
  96.9 1.2 %write_results.1 = (bf16[128,2048]{1,0:T(8,128)(2,1)}, f32[256,256]{1,0:T(8,128)}, f32[256,256]{1,0:T(8,128)}, f32[256,256]{1,0:T(8,128)}, f32[256,256]{1,0:T(8,128)}) custom-call(bf16[128,2048]{1,0:T(8,128)(2,1)S(1)} %get-tuple-element.10.refs_0_, f32[256,256]{1,0:T(8,128)S(1)} %get-tuple-element.11.refs_1_, f32[256,256]{1,0:T(8,128)S(1)} %get-tuple-element.12.refs_2_, ...), custom_call_target="tpu_custom_call" | custom-call | tf_op jit(solution)/shard_map/write_results/pallas_call | solution.py:603

commit v5 on v4

--- a/solution.py
+++ b/solution.py
@@ -74,7 +74,7 @@
         self.waiter(self.sends[send], 0, ref, peer).wait_send()
 
 
-N_GROUPS, N_SENDS = 63, 6
+N_GROUPS, N_SENDS = 75, 6
 
 
 def kernel(
@@ -311,56 +311,64 @@
                     part_z[u, zp(k), h, w, fy] = res[at : at + 64, fy * 256 : fy * 256 + 256]
 
     def ring_far(key, block, far, near, to, send):
-        net.start((key, 1), send, block(2, 0), far(0), to[1])
-        net.start((key, 3), send, block(2, 1), far(1), to[3])
-
-    def ring_near(k, key, block, far, near, to, send):
+        net.start((key, "far", 1), send, block(2, 0), far(0), to[1])
+        net.start((key, "far", 3), send, block(2, 1), far(1), to[3])
+
+    def ring_near(k, group, key, block, far, near, to, send):
         half, side = (1, 0) if k == 1 else (0, 1)
-        net.start(key, send, block(k, half), near(side, half), to[k])
-
-    def ring_both(k, add, key, block, far, near, to, send):
+        net.start(group, send, block(k, half), near(side, half), to[k])
+
+    def ring_both(k, group, key, block, far, near, to, send):
         half, side = (0, 0) if k == 1 else (1, 1)
-        arrived((key, k), far(side))
+        net.start(group, send, block(k, half), near(side, half), to[k])
+
+    def ring_add(k, add, key, block, far, near, to, send):
+        half, side = (0, 0) if k == 1 else (1, 1)
+        arrived((key, "far", k), far(side))
         add(block(k, half), far(side))
-        net.start(key, send, block(k, half), near(side, half), to[k])
 
     def add_into(dst, src):
         dst[...] = (dst[...].astype(F32) + src[...].astype(F32)).astype(BF)
 
-    def add_pair(dst, src):
-        for w in range(2):
+    def add_each(dst, src):
+        for w in range(dst.shape[0]):
             add_into(dst.at[w], src.at[w])
 
-    def first(u, pair):
+    splits = {0: [(0, 2)], 1: [(0, 1), (1, 1)]}
+
+    def first(u, pair, start=0, n=2):
+        ws = pl.ds(start, n)
         if pair == 0:
             return (
                 ("s1", u, pair),
-                lambda k, h: part_y.at[u, yp(k), h],
-                lambda s: far_y.at[u, s],
-                lambda s, h: near_y.at[u, s, h],
+                lambda k, h: part_y.at[u, yp(k), h, ws],
+                lambda s: far_y.at[u, s, ws],
+                lambda s, h: near_y.at[u, s, h, ws],
                 to_y,
                 "sums",
             )
         return (
             ("s1", u, pair),
-            lambda k, h: part_z.at[u, zp(k), h],
-            lambda s: far_z.at[u, s],
-            lambda s, h: near_z.at[u, s, h],
+            lambda k, h: part_z.at[u, zp(k), h, ws],
+            lambda s: far_z.at[u, s, ws],
+            lambda s, h: near_z.at[u, s, h, ws],
             to_z,
             "sums",
         )
 
-    def second(u, pair):
+    def second(u, pair, start, n):
+        ws = pl.ds(start, n)
+
         def block(k, h):
             if pair == 0:
-                return part_y.at[u, y, h, pl.ds(0, 2), zp(k) // 2, zp(k) % 2]
-            return part_z.at[u, z, h, pl.ds(0, 2), yp(k)]
+                return part_y.at[u, y, h, ws, zp(k) // 2, zp(k) % 2]
+            return part_z.at[u, z, h, ws, yp(k)]
 
         return (
-            ("s2", u, pair),
+            ("s2", u, pair, start),
             block,
-            lambda s: far2.at[u, pair, s],
-            lambda s, h: near2.at[u, pair, s, h],
+            lambda s: far2.at[u, pair, s, ws],
+            lambda s, h: near2.at[u, pair, s, h, ws],
             to_z if pair == 0 else to_y,
             "sums",
         )
@@ -371,37 +379,50 @@
 
     def grads_next(u, k):
         for pair in range(2):
-            ring_near(k, *first(u, pair))
+            ring_near(k, ("s1n", u, pair), *first(u, pair))
 
     def grads_b(u):
         for k in (1, 3):
             for pair in range(2):
-                ring_both(k, add_pair, *first(u, pair))
-
-    def grads_c(u):
+                ring_add(k, add_each, *first(u, pair))
+                start, n = splits[u][0]
+                ring_both(k, ("s1b", u, pair, start), *first(u, pair, start, n))
+        for start, n in splits[u][1:]:
+            for k in (1, 3):
+                for pair in range(2):
+                    ring_both(k, ("s1b", u, pair, start), *first(u, pair, start, n))
+
+    def grads_c(u, part):
+        start, n = splits[u][part]
         for pair in range(2):
             own, near = (part_y.at[u, y], near_y.at[u]) if pair == 0 else (part_z.at[u, z], near_z.at[u])
-            arrived(("s1", u, pair), near)
+            if part == 0:
+                arrived(("s1n", u, pair), near.at[0])
+            arrived(("s1b", u, pair, start), near.at[0] if n == 2 else near.at[0, 0])
             for h in range(2):
-                for w in range(2):
+                for w in range(start, start + n):
                     total = own[h, w].astype(F32) + near[0, h, w].astype(F32) + near[1, h, w].astype(F32)
                     own[h, w] = total.astype(BF)
-            ring_far(*second(u, pair))
-
-    def grads_near(u):
+            ring_far(*second(u, pair, start, n))
+
+    def grads_near(u, part):
         for pair in range(2):
             for k in (1, 3):
-                ring_near(k, *second(u, pair))
-
-    def grads_d(u):
+                args = second(u, pair, *splits[u][part])
+                ring_near(k, args[0], *args)
+
+    def grads_d(u, part):
         for k in (1, 3):
             for pair in range(2):
-                ring_both(k, add_into, *second(u, pair))
+                args = second(u, pair, *splits[u][part])
+                ring_add(k, add_into, *args)
+                ring_both(k, args[0], *args)
 
     def grads_e(u):
         for pair, outs in ((0, (go_ref, gv_ref)), (1, (gq_ref, gk_ref))):
             near = near2.at[u, pair]
-            arrived(("s2", u, pair), near)
+            for start, n in splits[u]:
+                arrived(("s2", u, pair, start), near if n == 2 else near.at[0])
             for w in range(2):
                 for h in range(2):
                     own = part_y[u, y, h, w, zh, zl] if pair == 0 else part_z[u, z, h, w, y]
@@ -521,29 +542,34 @@
     d_cross(3)
     weight_grads(0, 0)
     d_merge(1)
-    ring_near(1, *d_ring)
+    ring_near(1, "dx", *d_ring)
     d_merge(3)
-    ring_near(3, *d_ring)
-    grads_c(0)
+    ring_near(3, "dx", *d_ring)
+    grads_c(0, 0)
     grads_b(1)
-    grads_near(0)
     weight_grads(1, 0)
-    ring_both(1, d_add, *d_ring)
-    ring_both(3, d_add, *d_ring)
+    for k in (1, 3):
+        ring_add(k, d_add, *d_ring)
+        ring_both(k, "dx", *d_ring)
     d_tokens(0, [x])
     d_tokens(1, [x])
     d_cross(0)
-    grads_d(0)
     d_merge(0)
-    grads_c(1)
-    grads_near(1)
+    grads_c(1, 0)
+    grads_near(1, 0)
+    grads_near(0, 0)
+    grads_c(1, 1)
+    grads_near(1, 1)
+    grads_d(1, 0)
+    grads_d(0, 0)
+    grads_d(1, 1)
+    d_inputs()
     grads_e(0)
-    grads_d(1)
-    d_inputs()
     grads_e(1)
     w_all = wgt.at[pl.ds(0, 2), pl.ds(0, 4), pl.ds(0, 4), pl.ds(0, 4), pl.ds(0, 240)]
     rows_all = tok.at[pl.ds(0, 4), pl.ds(0, 2), pl.ds(0, 112)]
     sizes = {"w": w_all, "cot": rows_all, "tok": rows_all, "rel": rel.at[zh], "sums": w_all, "dn": rows_all}
+    assert len(net.groups) == N_GROUPS and len(net.sends) == N_SENDS
     for name, ref in sizes.items():
         net.sent(name, ref, sib)
 

time: 98.5 us -> 98 us (level)
  no operation moved by 1% of the time
where the time goes in v5:
time: 98 us; the launch traced here: 97.8 us
  Pallas kernels  97 us (99%)
    pallas_call x1, Pallas kernels, per_device(): pl.pallas_call(kernel, out_shape=tuple((pltpu.VMEM(s.shape, s.dtype) for...  95.8 us

profile of v5, /device:TPU:0, one launch (start us, length us, event | category | flops | bytes accessed | tf_op | source)
XLA Modules:
  0.0 97.8 jit_solution(13570736655915104737)
XLA Ops:
  0.6 95.8 %attention_backward.1 = (bf16[128,2048]{1,0:T(8,128)(2,1)S(1)}, f32[256,256]{1,0:T(8,128)S(1)}, f32[256,256]{1,0:T(8,128)S(1)}, f32[256,256]{1,0:T(8,128)S(1)}, f32[256,256]{1,0:T(8,128)S(1)}) custom-call(bf16[128,2048]{1,0:T(8,128)(2,1)} %x_in.1, f32[1,2048]{1,0:T(1,128)} %bitcast.1, bf16[256,256]{1,0:T(8,128)(2,1)} %wq_in.1, bf16[256,256]{1,0:T(8,128)(2,1)} %wk_in.1, ...), custom_call_target="tpu_custom_call" | custom-call | tf_op jit(solution)/shard_map/attention_backward/pallas_call | solution.py:590
  96.5 1.2 %write_results.1 = (bf16[128,2048]{1,0:T(8,128)(2,1)}, f32[256,256]{1,0:T(8,128)}, f32[256,256]{1,0:T(8,128)}, f32[256,256]{1,0:T(8,128)}, f32[256,256]{1,0:T(8,128)}) custom-call(bf16[128,2048]{1,0:T(8,128)(2,1)S(1)} %get-tuple-element.10.refs_0_, f32[256,256]{1,0:T(8,128)S(1)} %get-tuple-element.11.refs_1_, f32[256,256]{1,0:T(8,128)S(1)} %get-tuple-element.12.refs_2_, ...), custom_call_target="tpu_custom_call" | custom-call | tf_op jit(solution)/shard_map/write_results/pallas_call | solution.py:629

commit v6 on v5

--- a/solution.py
+++ b/solution.py
@@ -291,6 +291,10 @@
             dheads[u, KEY - 1, rows, lanes] = dk_t.T
 
     def weight_grads(u, k):
+        weight_grads_y(u, k)
+        weight_grads_z(u, k)
+
+    def weight_grads_y(u, k):
         cols = pl.ds(pl.multiple_of(yp(k) * 512, 512), 512)
         for w, buf in ((OUT, cot), (VAL, tok)):
             res = dot_nn(rows_t[u, w], buf[:, :, :, cols].reshape(1024, 512)).astype(BF)
@@ -299,6 +303,8 @@
                     at = g * 128 + h * 64
                     for fz in range(2):
                         part_y[u, yp(k), h, w, g, fz] = res[at : at + 64, fz * 256 : fz * 256 + 256]
+
+    def weight_grads_z(u, k):
         rows = pl.ds(pl.multiple_of(zp(k) // 2 * 128, 128), 128)
         left = jnp.concatenate([rows_t[u, w, rows] for w in (QRY, KEY)], axis=0)
         starts = [pl.multiple_of((fy * 2 + zp(k) % 2) * 256, 256) for fy in range(4)]
@@ -374,8 +380,10 @@
         )
 
     def grads_far(u):
-        for pair in range(2):
-            ring_far(*first(u, pair))
+        weight_grads_y(u, 2)
+        ring_far(*first(u, 0))
+        weight_grads_z(u, 2)
+        ring_far(*first(u, 1))
 
     def grads_next(u, k):
         for pair in range(2):
@@ -518,7 +526,6 @@
     passages(0, [xp(3)])
     arrived("far", tok.at[pl.ds(0, 2), 0])
     passages(0, [xp(2)])
-    weight_grads(0, 2)
     grads_far(0)
     for k in (1, 3):
         weight_grads(0, k)
@@ -528,7 +535,6 @@
     passages(1, [0, 1])
     grads_b(0)
     passages(1, [2, 3])
-    weight_grads(1, 2)
     grads_far(1)
     d_tokens(1, [xp(2)])
     d_cross(2)

time: 98 us -> 98.5 us (level)
  no operation moved by 1% of the time
where the time goes in v6:
time: 98.5 us; the launch traced here: 98.4 us
  Pallas kernels  97.6 us (99%)
    pallas_call x1, Pallas kernels, per_device(): pl.pallas_call(kernel, out_shape=tuple((pltpu.VMEM(s.shape, s.dtype) for...  96.4 us

profile of v6, /device:TPU:0, one launch (start us, length us, event | category | flops | bytes accessed | tf_op | source)
XLA Modules:
  0.0 98.4 jit_solution(17635978352498879933)
XLA Ops:
  0.6 96.4 %attention_backward.1 = (bf16[128,2048]{1,0:T(8,128)(2,1)S(1)}, f32[256,256]{1,0:T(8,128)S(1)}, f32[256,256]{1,0:T(8,128)S(1)}, f32[256,256]{1,0:T(8,128)S(1)}, f32[256,256]{1,0:T(8,128)S(1)}) custom-call(bf16[128,2048]{1,0:T(8,128)(2,1)} %x_in.1, f32[1,2048]{1,0:T(1,128)} %bitcast.1, bf16[256,256]{1,0:T(8,128)(2,1)} %wq_in.1, bf16[256,256]{1,0:T(8,128)(2,1)} %wk_in.1, ...), custom_call_target="tpu_custom_call" | custom-call | tf_op jit(solution)/shard_map/attention_backward/pallas_call | solution.py:596
  97.0 1.2 %write_results.1 = (bf16[128,2048]{1,0:T(8,128)(2,1)}, f32[256,256]{1,0:T(8,128)}, f32[256,256]{1,0:T(8,128)}, f32[256,256]{1,0:T(8,128)}, f32[256,256]{1,0:T(8,128)}) custom-call(bf16[128,2048]{1,0:T(8,128)(2,1)S(1)} %get-tuple-element.10.refs_0_, f32[256,256]{1,0:T(8,128)S(1)} %get-tuple-element.11.refs_1_, f32[256,256]{1,0:T(8,128)S(1)} %get-tuple-element.12.refs_2_, ...), custom_call_target="tpu_custom_call" | custom-call | tf_op jit(solution)/shard_map/write_results/pallas_call | solution.py:635
